TPU v7x, 32 devices: a whole 2x2x4 slice. The times are simulated.
32 devices in a mesh: dp: 8 (over z, x), mp: 4 (over y, core).
Axes of the slice: x: 2, y: 2, z: 4, core: 2. Of those that a mesh axis runs over, the one named last changes fastest.
Arguments:
- tokens: bfloat16 [12288, 768], P('dp'), may hold values from -6 to 6
- lengths: int32 [8, 2], P('dp'), may hold values from 0 to 1536, as said below
- w_query: bfloat16 [768, 768], P(None, 'mp'), may hold values from -0.21875 to 0.21875
- b_query: float32 [768], P('mp'), may hold values from -3 to 3
- w_key: bfloat16 [768, 768], P(None, 'mp'), may hold values from -0.21875 to 0.21875
- b_key: float32 [768], P('mp'), may hold values from -3 to 3
- w_value: bfloat16 [768, 768], P(None, 'mp'), may hold values from -0.21875 to 0.21875
- b_value: float32 [768], P('mp'), may hold values from -3 to 3
- w_out: bfloat16 [768, 768], P('mp'), may hold values from -1.75 to 1.75
- b_out: float32 [768], replicated, may hold values from -3 to 3
- ln1_gain: float32 [768], replicated, may hold values from 0.5 to 1.5
- ln1_bias: float32 [768], replicated, may hold values from -3 to 3
- w_in: bfloat16 [768, 3072], P('dp', 'mp'), may hold values from -0.21875 to 0.21875
- b_in: float32 [3072], P('mp'), may hold values from -3 to 3
- w_down: bfloat16 [3072, 768], P('mp', 'dp'), may hold values from -0.109375 to 0.109375
- b_down: float32 [768], replicated, may hold values from -3 to 3
- ln2_gain: float32 [768], replicated, may hold values from 0.5 to 1.5
- ln2_bias: float32 [768], replicated, may hold values from -3 to 3
- cotangent: float32 [12288, 768], P('dp'), may hold values from -6 to 6
Outputs:
- layer_out: bfloat16 [12288, 768], P('dp')
- grad_tokens: float32 [12288, 768], P('dp', 'mp')
- grad_w_query: float32 [768, 768], P(None, 'mp')
- grad_b_query: float32 [768], P('mp')
- grad_w_key: float32 [768, 768], P(None, 'mp')
- grad_b_key: float32 [768], P('mp')
- grad_w_value: float32 [768, 768], P(None, 'mp')
- grad_b_value: float32 [768], P('mp')
- grad_w_out: float32 [768, 768], P('mp')
- grad_b_out: float32 [768], replicated
- grad_ln1_gain: float32 [768], replicated
- grad_ln1_bias: float32 [768], replicated
- grad_w_in: float32 [768, 3072], P('dp', 'mp')
- grad_b_in: float32 [3072], P('mp')
- grad_w_down: float32 [3072, 768], P('mp', 'dp')
- grad_b_down: float32 [768], replicated
- grad_ln2_gain: float32 [768], replicated
- grad_ln2_bias: float32 [768], replicated
Inputs may be any that keep to these rules, and one draw needn't show every extreme that they name: Row r holds a sequence of lengths[r, 0] tokens from slot 0, at least 64, then a second sequence of lengths[r, 1] tokens (0, or at least 64), then padding; lengths[r, 0] + lengths[r, 1] <= 1536; some row holds one sequence of all 1536 slots.
All inputs are finite; a program needn't handle non-finite values.
Results may differ from a plain program's by a relative error of at most 0.03.
Values may be sent and summed in bfloat16 or wider, within the bound.
No kernel may reach another device: no remote copies, remote signals or barrier semaphores. Data moves between devices by JAX's collectives and lax.ppermute only.
A program may use at most 192 MiB of HBM per device.

v0:
```python
from functools import partial
import math

import jax
import jax.numpy as jnp
from jax import lax
from jax.sharding import PartitionSpec as P

HEAD_DIM = 64


norm_eps = 1e-12
masked_score = -1e30


def layer_norm(summed, gain_vec, shift_vec):
    center = summed - jnp.mean(summed, axis=-1, keepdims=True)
    spread = jnp.mean(center * center, axis=-1, keepdims=True)
    return center * lax.rsqrt(spread + norm_eps) * gain_vec + shift_vec


def rotary_tables(lengths, slot_count, head_width):
    places = jnp.arange(slot_count, dtype=jnp.int32)[None, :]
    first_len = lengths[:, 0:1]
    used_len = first_len + lengths[:, 1:2]
    segment = (places >= first_len).astype(jnp.int32) + (places >= used_len).astype(jnp.int32)
    starts = jnp.where(segment == 0, 0, jnp.where(segment == 1, first_len, used_len))
    offsets = (places - starts).astype(jnp.float32)
    halfdim = head_width // 2
    frequency = jnp.exp(jnp.arange(halfdim, dtype=jnp.float32) * (-math.log(10000.0) / halfdim))
    frequency = jnp.concatenate([frequency, frequency])
    angles = offsets[:, :, None, None] * frequency
    return (segment, jnp.cos(angles), jnp.sin(angles))


def rotate(vectors, cosine_tab, sine_tab):
    halfdim = vectors.shape[-1] // 2
    turned = jnp.concatenate([-vectors[..., halfdim:], vectors[..., :halfdim]], axis=-1)
    return vectors * cosine_tab + turned * sine_tab


def rotate_back(grads, cosine_tab, sine_tab):
    halfdim = grads.shape[-1] // 2
    turned = grads * sine_tab
    return grads * cosine_tab + jnp.concatenate(
        [turned[..., halfdim:], -turned[..., :halfdim]], axis=-1
    )


def score_block(query_blk, seg_query, keyset, seg_keys, score_scale):
    scores = (
        jnp.einsum("qhd,khd->hqk", query_blk, keyset, preferred_element_type=jnp.float32)
        * score_scale
    )
    allowed = (seg_query[:, None] == seg_keys[None, :])[None]
    return jnp.where(allowed, scores, masked_score)


def contract_rows(left_mat, right_mat):
    return lax.dot_general(
        left_mat, right_mat, (((0,), (0,)), ((), ())), preferred_element_type=jnp.float32
    )


def contract_cols(left_mat, right_mat):
    return lax.dot_general(
        left_mat, right_mat, (((1,), (1,)), ((), ())), preferred_element_type=jnp.float32
    )


def shards(
    tokens,
    lengths,
    w_query,
    b_query,
    w_key,
    b_key,
    w_value,
    b_value,
    w_out,
    b_out,
    ln1_gain,
    ln1_bias,
    w_in,
    b_in,
    w_down,
    b_down,
    ln2_gain,
    ln2_bias,
    cotangent,
):
    row_count = lengths.shape[0]
    tok_count = tokens.shape[0]
    slot_count = tok_count // row_count
    model_width = tokens.shape[1]
    local_width = w_query.shape[1]
    head_count = local_width // HEAD_DIM
    block_rows = min(512, slot_count)
    block_count = slot_count // block_rows
    score_scale = 1.0 / math.sqrt(HEAD_DIM)
    segment, cosine_tab, sine_tab = rotary_tables(lengths, slot_count, HEAD_DIM)
    head_shape = (row_count, slot_count, head_count, HEAD_DIM)
    block_shape = (block_count, block_rows, head_count, HEAD_DIM)

    def project(weight, shift_vec):
        return jnp.dot(tokens, weight, preferred_element_type=jnp.float32) + shift_vec

    queries = rotate(project(w_query, b_query).reshape(head_shape), cosine_tab, sine_tab).astype(
        jnp.bfloat16
    )
    keyset = rotate(project(w_key, b_key).reshape(head_shape), cosine_tab, sine_tab).astype(
        jnp.bfloat16
    )
    values = project(w_value, b_value).astype(jnp.bfloat16).reshape(head_shape)
    index_row = 0
    row_k = keyset[index_row]
    row_v = values[index_row]
    row_seg = segment[index_row]

    def one_block(block_items):
        query_blk, seg_query = block_items
        scores = score_block(query_blk, seg_query, row_k, row_seg, score_scale)
        top_score = jnp.max(scores, axis=-1, keepdims=True)
        exp_scores = jnp.exp(scores - top_score)
        denominator = jnp.sum(exp_scores, axis=-1, keepdims=True)
        probability = (exp_scores / denominator).astype(jnp.bfloat16)
        mixed_blk = jnp.einsum(
            "hqk,khd->qhd", probability, row_v, preferred_element_type=jnp.float32
        )
        return (mixed_blk, top_score, denominator)

    mixed_blocks, top_blocks, denom_blocks = lax.map(
        one_block,
        (queries[index_row].reshape(block_shape), row_seg.reshape(block_count, block_rows)),
    )
    mixed_rows = [mixed_blocks]
    top_rows = [top_blocks]
    denom_rows = [denom_blocks]
    attn_mix = jnp.stack(mixed_rows).reshape(tok_count, local_width).astype(jnp.bfloat16)
    attended = lax.psum(
        jnp.dot(attn_mix, w_out, preferred_element_type=jnp.float32).astype(jnp.bfloat16), "mp"
    ).astype(jnp.float32)
    pre_one = tokens.astype(jnp.float32) + attended + b_out
    normed_one, norm_one_back = jax.vjp(layer_norm, pre_one, ln1_gain, ln1_bias)
    tile_in, tile_down = (
        lax.all_gather(w_in, "dp", axis=0, tiled=True),
        lax.all_gather(w_down, "dp", axis=1, tiled=True),
    )
    normed_low = normed_one.astype(jnp.bfloat16)
    inner_pre = jnp.dot(normed_low, tile_in, preferred_element_type=jnp.float32) + b_in
    active, gelu_back = jax.vjp(partial(jax.nn.gelu, approximate=False), inner_pre)
    active_low = active.astype(jnp.bfloat16)
    result = lax.psum(
        jnp.dot(active_low, tile_down, preferred_element_type=jnp.float32).astype(jnp.bfloat16),
        "mp",
    ).astype(jnp.float32)
    layer_out, norm_two_back = jax.vjp(layer_norm, normed_one + result + b_down, ln2_gain, ln2_bias)
    valid_rows = (segment < 2).reshape(tok_count, 1)
    grad_out = jnp.where(valid_rows, cotangent, 0.0)
    grad_sum_two, grad_ln2_gain, grad_ln2_bias = norm_two_back(grad_out)
    grad_b_down = jnp.sum(grad_sum_two, axis=0)
    grad_result = grad_sum_two.astype(jnp.bfloat16)
    back_in, back_down = (
        lax.all_gather(w_in, "dp", axis=0, tiled=True),
        lax.all_gather(w_down, "dp", axis=1, tiled=True),
    )
    grad_active = contract_cols(grad_result, back_down)
    grad_inner = gelu_back(grad_active)[0].astype(jnp.bfloat16)
    grad_b_in = jnp.sum(grad_inner, axis=0, dtype=jnp.float32)
    columns = normed_low
    grad_w_in = lax.psum_scatter(
        contract_rows(columns, grad_inner), "dp", scatter_dimension=0, tiled=True
    )
    columns = lax.slice_in_dim(grad_result, 0, lax.axis_size("dp") * w_down.shape[1], axis=1)
    grad_w_down = lax.psum_scatter(
        contract_rows(columns, active_low), "dp", scatter_dimension=0, tiled=True
    ).T
    ffn_part = contract_cols(grad_inner, back_in)
    grad_normed = grad_sum_two + lax.psum(ffn_part.astype(jnp.bfloat16), "mp").astype(jnp.float32)
    grad_sum_one, grad_ln1_gain, grad_ln1_bias = norm_one_back(grad_normed)
    grad_b_out = jnp.sum(grad_sum_one, axis=0)
    grad_attended = grad_sum_one.astype(jnp.bfloat16)
    grad_w_out = contract_rows(attn_mix, grad_attended)
    grad_mix = contract_cols(grad_attended, w_out).astype(jnp.bfloat16).reshape(head_shape)
    index_row = 0
    attend_row_k = keyset[index_row]
    attend_row_v = values[index_row]
    attend_row_seg = segment[index_row]

    def one_block(carry, block_items):
        grad_keys, grad_values = carry
        query_blk, seg_query, grad_blk, top_score, denominator = block_items
        scores = score_block(query_blk, seg_query, attend_row_k, attend_row_seg, score_scale)
        probability = jnp.exp(scores - top_score) / denominator
        grad_prob = jnp.einsum(
            "qhd,khd->hqk", grad_blk, attend_row_v, preferred_element_type=jnp.float32
        )
        delta = jnp.sum(probability * grad_prob, axis=-1, keepdims=True)
        grad_scores = (probability * (grad_prob - delta)).astype(jnp.bfloat16)
        grad_query = (
            jnp.einsum(
                "hqk,khd->qhd", grad_scores, attend_row_k, preferred_element_type=jnp.float32
            )
            * score_scale
        )
        grad_keys = (
            grad_keys
            + jnp.einsum("hqk,qhd->khd", grad_scores, query_blk, preferred_element_type=jnp.float32)
            * score_scale
        )
        grad_values = grad_values + jnp.einsum(
            "hqk,qhd->khd",
            probability.astype(jnp.bfloat16),
            grad_blk,
            preferred_element_type=jnp.float32,
        )
        return ((grad_keys, grad_values), grad_query)

    zero_grads = jnp.zeros((slot_count, head_count, HEAD_DIM), jnp.float32)
    (grad_keys, grad_values), grad_queries = lax.scan(
        one_block,
        (zero_grads, zero_grads),
        (
            queries[index_row].reshape(block_shape),
            attend_row_seg.reshape(block_count, block_rows),
            grad_mix[index_row].reshape(block_shape),
            top_rows[index_row],
            denom_rows[index_row],
        ),
    )
    grad_q_row = grad_queries.reshape(slot_count, head_count, HEAD_DIM)
    query_grads = [grad_q_row]
    key_grads = [grad_keys]
    value_grads = [grad_values]
    grad_query_lin = (
        rotate_back(jnp.stack(query_grads), cosine_tab, sine_tab)
        .reshape(tok_count, local_width)
        .astype(jnp.bfloat16)
    )
    grad_key_lin = (
        rotate_back(jnp.stack(key_grads), cosine_tab, sine_tab)
        .reshape(tok_count, local_width)
        .astype(jnp.bfloat16)
    )
    grad_value_lin = jnp.stack(value_grads).reshape(tok_count, local_width).astype(jnp.bfloat16)
    grad_w_query = contract_rows(tokens, grad_query_lin)
    grad_w_key = contract_rows(tokens, grad_key_lin)
    grad_w_value = contract_rows(tokens, grad_value_lin)
    grad_b_query = jnp.sum(grad_query_lin, axis=0, dtype=jnp.float32)
    grad_b_key = jnp.sum(grad_key_lin, axis=0, dtype=jnp.float32)
    grad_b_value = jnp.sum(grad_value_lin, axis=0, dtype=jnp.float32)
    input_part = (
        contract_cols(grad_query_lin, w_query)
        + contract_cols(grad_key_lin, w_key)
        + contract_cols(grad_value_lin, w_value)
    )
    share_width = model_width // lax.axis_size("mp")
    share_start = lax.axis_index("mp") * share_width
    summed_all = lax.psum(input_part.astype(jnp.bfloat16), "mp").astype(jnp.float32)
    grad_tokens = lax.dynamic_slice_in_dim(summed_all, share_start, share_width, 1)
    grad_tokens = grad_tokens + lax.dynamic_slice_in_dim(grad_sum_one, share_start, share_width, 1)
    (
        grad_w_query,
        grad_b_query,
        grad_w_key,
        grad_b_key,
        grad_w_value,
        grad_b_value,
        grad_w_out,
        grad_b_out,
        grad_ln1_gain,
        grad_ln1_bias,
        grad_b_in,
        grad_b_down,
        grad_ln2_gain,
        grad_ln2_bias,
    ) = lax.psum(
        (
            grad_w_query,
            grad_b_query,
            grad_w_key,
            grad_b_key,
            grad_w_value,
            grad_b_value,
            grad_w_out,
            grad_b_out,
            grad_ln1_gain,
            grad_ln1_bias,
            grad_b_in,
            grad_b_down,
            grad_ln2_gain,
            grad_ln2_bias,
        ),
        "dp",
    )
    return (
        layer_out.astype(jnp.bfloat16),
        grad_tokens,
        grad_w_query,
        grad_b_query,
        grad_w_key,
        grad_b_key,
        grad_w_value,
        grad_b_value,
        grad_w_out,
        grad_b_out,
        grad_ln1_gain,
        grad_ln1_bias,
        grad_w_in,
        grad_b_in,
        grad_w_down,
        grad_b_down,
        grad_ln2_gain,
        grad_ln2_bias,
    )


def solution(mesh):
    in_specs = (
        P("dp", None),
        P("dp", None),
        P(None, "mp"),
        P("mp"),
        P(None, "mp"),
        P("mp"),
        P(None, "mp"),
        P("mp"),
        P("mp", None),
        P(),
        P(),
        P(),
        P("dp", "mp"),
        P("mp"),
        P("mp", "dp"),
        P(),
        P(),
        P(),
        P("dp", None),
    )
    out_specs = (
        P("dp", None),
        P("dp", "mp"),
        P(None, "mp"),
        P("mp"),
        P(None, "mp"),
        P("mp"),
        P(None, "mp"),
        P("mp"),
        P("mp", None),
        P(),
        P(),
        P(),
        P("dp", "mp"),
        P("mp"),
        P("mp", "dp"),
        P(),
        P(),
        P(),
    )
    return jax.shard_map(shards, mesh=mesh, in_specs=in_specs, out_specs=out_specs, check_vma=False)
```

profile of v0, /device:TPU:0, one launch (start us, length us, event | category | flops | bytes accessed | tf_op | source)
XLA Modules:
  0.0 678.5 jit_solution(17987873459520155300)
XLA Ops:
  19.4 4.6 multiply_cosine_fusion
  43.0 33.4 %while.30 = (s32[]{:T(128)}, bf16[3,512,3,64]{1,3,2,0:T(8,128)(2,1)}, f32[3,3,512,1]{2,1,3,0:T(4,128)S(1)}, f32[3,3,512,1]{2,1,3,0:T(4,128)S(1)}, s32[3,512]{1,0...) while((s32[]{:T(128)}, ...), condition=%wide.region_3.4_spmd.clone, body=%wide.region_0.3_spmd.clone.sunk | while | flops 633082368 | bytes 35669144 | solution.py:132
  50.0 4.2 fusion.153
  61.1 4.2 fusion.153
  72.3 4.2 fusion.153
  82.9 56.9 %all-reduce.8.cloned.1.call-done = bf16[1536,768]{1,0:T(8,128)(2,1)} async-done(((bf16[1536,768]{1,0:T(8,128)(2,1)}), bf16[1536,768]{1,0:T(8,128)(2,1)}) %all-reduce.8.cloned.1.call-update) | async-done | bytes 2359312 | tf_op jit(solution)/shard_map/psum | solution.py:140
  143.9 15.8 %multiply_convert_fusion.1 = (bf16[1536,768]{1,0:T(8,128)(2,1)}, f32[1536,768]{1,0:T(8,128)}, f32[1536,768]{1,0:T(8,128)}) fusion(f32[768]{0:T(1024)S(1)} %copy-done.57, bf16[768,768]{1,0:T(8,128)(2,1)} %all-gather.3.cloned.1.call-done, f32[768]{0:T(1024)S(1)} %copy-done.50, f32[768]{0:T(1024)S(1)} %copy-done.38, f32[1536]{0:T(1024)S(1)} %fusion.70, ...), kind=kOutput, calls=%fused_computation.72 | convolution fusion | flops 1900412928 | bytes 17719296 | tf_op jit(solution)/shard_map/dot_general | solution.py:150
  159.7 10.3 %all-gather.5.cloned.1.call-done = bf16[768,768]{0,1:T(8,128)(2,1)} async-done(((bf16[768,96]{0,1:T(8,128)(2,1)}), bf16[768,768]{0,1:T(8,128)(2,1)}) %all-gather.5.cloned.1.call-update) | async-done | bytes 1179664 | tf_op jit(solution)/shard_map/all_gather | solution.py:147
  170.0 5.4 convolution_convert_fusion.1
  176.2 53.6 %all-reduce.10.cloned.1.call-done = bf16[1536,768]{1,0:T(8,128)(2,1)} async-done(((bf16[1536,768]{1,0:T(8,128)(2,1)}), bf16[1536,768]{1,0:T(8,128)(2,1)}) %all-reduce.10.cloned.1.call-update) | async-done | bytes 2359312 | tf_op jit(solution)/shard_map/psum | solution.py:153
  234.7 4.7 multiply_reduce_fusion.1
  243.2 4.3 convert_reduce_fusion
  252.6 55.6 %all-reduce.12.cloned.1.call-done = bf16[1536,768]{1,0:T(8,128)(2,1)} async-done(((bf16[1536,768]{1,0:T(8,128)(2,1)}), bf16[1536,768]{1,0:T(8,128)(2,1)}) %all-reduce.12.cloned.1.call-update) | async-done | bytes 2359312 | tf_op jit(solution)/shard_map/psum | solution.py:179
  308.3 5.9 fusion.81
  328.9 127.8 %while.31 = (s32[]{:T(128)}, f32[1536,3,64]{0,2,1:T(8,128)S(1)}, f32[1536,3,64]{0,2,1:T(8,128)S(1)}, f32[3,512,3,64]{1,0,3,2:T(4,128)}, bf16[3,512,3,64]{1,3,2,0...) while((s32[]{:T(128)}, f32[1536,3,64]{0,2,1:T(8,128)S(1)}, ...), condition=%wide.region_17.18_spmd.clone, body=%wide.region_15.17_spmd.clone.sunk | while | flops 1535907840 | bytes 119410880 | solution.py:220
  332.8 7.4 %multiply_reduce_fusion.8 = (f32[3,512]{1,0:T(4,128)S(1)}, f32[3,512,1536]{2,1,0:T(8,128)}) fusion(f32[3,512,1536]{2,1,0:T(8,128)S(1)} %fusion.163, f32[3,512]{1,0:T(4,128)S(1)} %get-tuple-element.540, f32[3,512]{1,0:T(4,128)S(1)} %get-tuple-element.541, bf16[1536,3,64]{0,2,1:T(8,128)(2,1)S(1)} %get-tuple-element.613, ...), kind=kOutput, calls=%fused_computation.25.clone.1 | convolution fusion | flops 316144128 | bytes 20466176 | tf_op jit(solution)/shard_map/while/body/eval_jaxpr/qhd,khd->hqk/dot_general | solution.py:52
  340.2 9.3 %multiply_convert_fusion.3 = bf16[3,512,1536]{2,1,0:T(8,128)(2,1)} fusion(f32[3,512,1536]{2,1,0:T(8,128)} %get-tuple-element.542, f32[3,512,1536]{2,1,0:T(8,128)} %copy-done.2, f32[3,512]{1,0:T(4,128)S(1)} %get-tuple-element.543), kind=kLoop, calls=%fused_computation.24.clone.1 | loop fusion | flops 7077888 | bytes 23599104 | tf_op jit(solution)/shard_map/while/body/eval_jaxpr/convert_element_type | solution.py:199
  354.6 8.6 %dynamic_update_slice.26 = f32[3,512,3,64]{1,0,3,2:T(4,128)} dynamic-update-slice(f32[3,512,3,64]{1,0,3,2:T(4,128)} %get-tuple-element.595, f32[1,512,3,64]{1,0,3,2:T(1,128)} %copy.80, s32[]{:T(128)} %get-tuple-element.592, s32[]{:T(128)} %constant.68.clone.1..sunk, s32[]{:T(128)} %constant.68.clone.1..sunk, s32[]{:T(128)} %constant.68.clone.1..sunk) | dynamic-update-slice | bytes 786436 | tf_op jit(solution)/shard_map/while/body/jit(dynamic_update_index_in_dim)/dynamic_update_slice | solution.py:132
  366.7 4.9 fusion.166
  375.4 7.4 %multiply_reduce_fusion.8 = (f32[3,512]{1,0:T(4,128)S(1)}, f32[3,512,1536]{2,1,0:T(8,128)}) fusion(f32[3,512,1536]{2,1,0:T(8,128)S(1)} %fusion.163, f32[3,512]{1,0:T(4,128)S(1)} %get-tuple-element.540, f32[3,512]{1,0:T(4,128)S(1)} %get-tuple-element.541, bf16[1536,3,64]{0,2,1:T(8,128)(2,1)S(1)} %get-tuple-element.613, ...), kind=kOutput, calls=%fused_computation.25.clone.1 | convolution fusion | flops 316144128 | bytes 20466176 | tf_op jit(solution)/shard_map/while/body/eval_jaxpr/qhd,khd->hqk/dot_general | solution.py:52
  382.8 9.3 %multiply_convert_fusion.3 = bf16[3,512,1536]{2,1,0:T(8,128)(2,1)} fusion(f32[3,512,1536]{2,1,0:T(8,128)} %get-tuple-element.542, f32[3,512,1536]{2,1,0:T(8,128)} %copy-done.2, f32[3,512]{1,0:T(4,128)S(1)} %get-tuple-element.543), kind=kLoop, calls=%fused_computation.24.clone.1 | loop fusion | flops 7077888 | bytes 23599104 | tf_op jit(solution)/shard_map/while/body/eval_jaxpr/convert_element_type | solution.py:199
  397.2 8.6 %dynamic_update_slice.26 = f32[3,512,3,64]{1,0,3,2:T(4,128)} dynamic-update-slice(f32[3,512,3,64]{1,0,3,2:T(4,128)} %get-tuple-element.595, f32[1,512,3,64]{1,0,3,2:T(1,128)} %copy.80, s32[]{:T(128)} %get-tuple-element.592, s32[]{:T(128)} %constant.68.clone.1..sunk, s32[]{:T(128)} %constant.68.clone.1..sunk, s32[]{:T(128)} %constant.68.clone.1..sunk) | dynamic-update-slice | bytes 786436 | tf_op jit(solution)/shard_map/while/body/jit(dynamic_update_index_in_dim)/dynamic_update_slice | solution.py:132
  409.3 4.9 fusion.166
  418.1 7.4 %multiply_reduce_fusion.8 = (f32[3,512]{1,0:T(4,128)S(1)}, f32[3,512,1536]{2,1,0:T(8,128)}) fusion(f32[3,512,1536]{2,1,0:T(8,128)S(1)} %fusion.163, f32[3,512]{1,0:T(4,128)S(1)} %get-tuple-element.540, f32[3,512]{1,0:T(4,128)S(1)} %get-tuple-element.541, bf16[1536,3,64]{0,2,1:T(8,128)(2,1)S(1)} %get-tuple-element.613, ...), kind=kOutput, calls=%fused_computation.25.clone.1 | convolution fusion | flops 316144128 | bytes 20466176 | tf_op jit(solution)/shard_map/while/body/eval_jaxpr/qhd,khd->hqk/dot_general | solution.py:52
  425.5 9.3 %multiply_convert_fusion.3 = bf16[3,512,1536]{2,1,0:T(8,128)(2,1)} fusion(f32[3,512,1536]{2,1,0:T(8,128)} %get-tuple-element.542, f32[3,512,1536]{2,1,0:T(8,128)} %copy-done.2, f32[3,512]{1,0:T(4,128)S(1)} %get-tuple-element.543), kind=kLoop, calls=%fused_computation.24.clone.1 | loop fusion | flops 7077888 | bytes 23599104 | tf_op jit(solution)/shard_map/while/body/eval_jaxpr/convert_element_type | solution.py:199
  439.8 8.6 %dynamic_update_slice.26 = f32[3,512,3,64]{1,0,3,2:T(4,128)} dynamic-update-slice(f32[3,512,3,64]{1,0,3,2:T(4,128)} %get-tuple-element.595, f32[1,512,3,64]{1,0,3,2:T(1,128)} %copy.80, s32[]{:T(128)} %get-tuple-element.592, s32[]{:T(128)} %constant.68.clone.1..sunk, s32[]{:T(128)} %constant.68.clone.1..sunk, s32[]{:T(128)} %constant.68.clone.1..sunk) | dynamic-update-slice | bytes 786436 | tf_op jit(solution)/shard_map/while/body/jit(dynamic_update_index_in_dim)/dynamic_update_slice | solution.py:132
  451.9 4.9 fusion.166
  477.5 6.8 fusion.72
  484.6 6.6 fusion.74
  497.7 38.1 %all-reduce = (f32[192]{0:T(256)}, f32[192]{0:T(256)}, f32[192]{0:T(256)}, f32[768]{0:T(1024)}, f32[768]{0:T(1024)}, /*index=5*/f32[768]{0:T(1024)}, f32[768]{0:...) all-reduce(f32[192]{0:T(256)S(1)} %reduce_sum.227, ...), channel_id=1, replica_groups=mesh['dp'=8,'mp'=4] {'dp'}, use_global_device_ids=true, to_apply=%region_21.22 | all-reduce | flops 5952 | bytes 47616 | tf_op jit(solution)/shard_map/psum | solution.py:277
  540.0 115.9 %all-reduce.16.cloned.1.call-done = (f32[768,192]{0,1:T(8,128)}, f32[768,192]{0,1:T(8,128)}, f32[768,192]{0,1:T(8,128)}, f32[192,768]{1,0:T(8,128)}) async-done(((f32[768,192]{0,1:T(8,128)}, f32[768,192]{0,1:T(8,128)}, f32[768,192]{0,1:T(8,128)}, f32[192,768]{1,0:T(8,128)}), (f32[768,192]{0,1:T(8,128)}, f32[768,192]{0,1:T(8,128)}, f32[768,192]{0,1:T(8,128)}, ...) | async-done | bytes 2359312 | tf_op jit(solution)/shard_map/psum | solution.py:277
  655.9 7.1 %reduce-scatter.3.cloned.1.call-done = f32[96,768]{1,0:T(8,128)} async-done(((f32[768,768]{1,0:T(8,128)}), f32[96,768]{1,0:T(8,128)}) %reduce-scatter.3.cloned.1.call-update) | async-done | bytes 294928 | tf_op jit(solution)/shard_map/reduce_scatter | solution.py:171
  (286 shorter events, 165.0 us)
Async XLA Ops:
  8.0 71.0 %copy-start = (bf16[192,768]{1,0:T(8,128)(2,1)S(1)}, bf16[192,768]{1,0:T(8,128)(2,1)}, u32[]{:S(2)}) copy-start(bf16[192,768]{1,0:T(8,128)(2,1)} %param.31) | copy-start | bytes 884740
  8.0 131.8 %all-reduce.8.cloned.1.call-start = ((), (), s32[]{:S(2)}) async-start(), calls=%async_computation.2 | async-start | bytes 4718592 | tf_op jit(solution)/shard_map/psum | solution.py:140
  12.1 11.9 %copy-start.3 = (bf16[1536,768]{1,0:T(8,128)(2,1)S(1)}, bf16[1536,768]{1,0:T(8,128)(2,1)}, u32[]{:S(2)}) copy-start(bf16[1536,768]{1,0:T(8,128)(2,1)} %param.23) | copy-start | bytes 7077892
  12.1 11.9 %copy-start.28 = (bf16[768,192]{0,1:T(8,128)(2,1)S(1)}, bf16[768,192]{0,1:T(8,128)(2,1)}, u32[]{:S(2)}) copy-start(bf16[768,192]{0,1:T(8,128)(2,1)} %param.25) | copy-start | bytes 884740
  12.1 11.9 %copy-start.52 = (f32[192]{0:T(256)S(1)}, f32[192]{0:T(256)}, u32[]{:S(2)}) copy-start(f32[192]{0:T(256)} %param.26) | copy-start | bytes 2308
  24.1 11.9 %copy-start.24 = (f32[3,512,64]{1,0,2:T(4,128)}, f32[3,512,64]{1,0,2:T(4,128)S(1)}, u32[]{:S(2)}) copy-start(f32[3,512,64]{1,0,2:T(4,128)S(1)} %get-tuple-element.379) | copy-start | bytes 1179652
  31.2 8.3 %copy-start.32 = (bf16[768,192]{0,1:T(8,128)(2,1)S(1)}, bf16[768,192]{0,1:T(8,128)(2,1)}, u32[]{:S(2)}) copy-start(bf16[768,192]{0,1:T(8,128)(2,1)} %param.29) | copy-start | bytes 884740
  31.2 8.3 %copy-start.58 = (f32[192]{0:T(256)S(1)}, f32[192]{0:T(256)}, u32[]{:S(2)}) copy-start(f32[192]{0:T(256)} %param.30) | copy-start | bytes 2308
  76.5 63.3 %copy-start.34 = (f32[768]{0:T(1024)S(1)}, f32[768]{0:T(1024)}, u32[]{:S(2)}) copy-start(f32[768]{0:T(1024)} %param.32) | copy-start | bytes 9220
  81.3 62.5 %all-gather.3.cloned.1.call-start = ((), (), s32[]{:S(2)}) async-start(), calls=%async_computation.3 | async-start | bytes 1327104 | tf_op jit(solution)/shard_map/all_gather | solution.py:146
  81.9 88.1 %all-gather.5.cloned.1.call-start = ((), (), s32[]{:S(2)}) async-start(), calls=%async_computation.4 | async-start | bytes 1327104 | tf_op jit(solution)/shard_map/all_gather | solution.py:147
  82.5 61.4 %copy-start.38 = (f32[768]{0:T(1024)S(1)}, f32[768]{0:T(1024)}, u32[]{:S(2)}) copy-start(f32[768]{0:T(1024)} %param.33) | copy-start | bytes 9220
  82.5 61.4 %copy-start.50 = (f32[768]{0:T(1024)S(1)}, f32[768]{0:T(1024)}, u32[]{:S(2)}) copy-start(f32[768]{0:T(1024)} %param.34) | copy-start | bytes 9220
  82.5 61.4 %copy-start.57 = (f32[768]{0:T(1024)S(1)}, f32[768]{0:T(1024)}, u32[]{:S(2)}) copy-start(f32[768]{0:T(1024)} %param.36) | copy-start | bytes 9220
  82.5 147.3 %all-reduce.10.cloned.1.call-start = ((), (), s32[]{:S(2)}) async-start(), calls=%async_computation.5 | async-start | bytes 4718592 | tf_op jit(solution)/shard_map/psum | solution.py:153
  142.5 175.2 %copy-start.30 = (f32[1536]{0:T(1024)}, f32[1536]{0:T(1024)S(1)}, u32[]{:S(2)}) copy-start(f32[1536]{0:T(1024)S(1)} %broadcast_multiply_fusion.2) | copy-start | bytes 18436
  143.8 173.9 %copy-start.36 = (f32[1536]{0:T(1024)}, f32[1536]{0:T(1024)S(1)}, u32[]{:S(2)}) copy-start(f32[1536]{0:T(1024)S(1)} %fusion.70) | copy-start | bytes 18436
  170.0 59.8 %copy-start.49 = (f32[768]{0:T(1024)S(1)}, f32[768]{0:T(1024)}, u32[]{:S(2)}) copy-start(f32[768]{0:T(1024)} %param.38) | copy-start | bytes 9220
  175.5 132.8 %all-reduce.12.cloned.1.call-start = ((), (), s32[]{:S(2)}) async-start(), calls=%async_computation.6 | async-start | bytes 4718592 | tf_op jit(solution)/shard_map/psum | solution.py:179
  234.7 8.4 %slice-start.4 = ((s8[4718592]{0:T(1024)(128)(4,1)}), s8[4194304]{0:T(1024)(128)(4,1)S(1)}, s32[]{:S(2)}) async-start(s8[4718592]{0:T(1024)(128)(4,1)} %bitcast.207), calls=%async_computation.15 | async-start | bytes 8388608
  234.7 8.4 %slice-start.6 = ((s8[4718592]{0:T(1024)(128)(4,1)}), s8[4194304]{0:T(1024)(128)(4,1)S(1)}, s32[]{:S(2)}) async-start(s8[4718592]{0:T(1024)(128)(4,1)} %bitcast.209), calls=%async_computation.17 | async-start | bytes 8388608
  243.1 65.2 %copy-start.40 = (f32[1536]{0:T(1024)}, f32[1536]{0:T(1024)S(1)}, u32[]{:S(2)}) copy-start(f32[1536]{0:T(1024)S(1)} %negate_multiply_fusion.2) | copy-start | bytes 18436
  252.4 283.4 %all-reduce.14.cloned.1.call-start = ((), (), s32[]{:S(2)}) async-start(), calls=%async_computation.7 | async-start | bytes 4718592 | tf_op jit(solution)/shard_map/psum | solution.py:259
  320.6 8.3 %copy-start.9 = (f32[1536,3,64]{0,2,1:T(8,128)S(1)}, f32[1536,3,64]{0,2,1:T(8,128)}, u32[]{:S(2)}) copy-start(f32[1536,3,64]{0,2,1:T(8,128)} %custom-call.1) | copy-start | bytes 3538948
  331.5 8.7 %copy-start.2 = (f32[3,512,1536]{2,1,0:T(8,128)}, f32[3,512,1536]{2,1,0:T(8,128)S(1)}, u32[]{:S(2)}) copy-start(f32[3,512,1536]{2,1,0:T(8,128)S(1)} %fusion.163) | copy-start | bytes 28311556 | tf_op jit(solution)/shard_map/while
  374.2 8.7 %copy-start.2 = (f32[3,512,1536]{2,1,0:T(8,128)}, f32[3,512,1536]{2,1,0:T(8,128)S(1)}, u32[]{:S(2)}) copy-start(f32[3,512,1536]{2,1,0:T(8,128)S(1)} %fusion.163) | copy-start | bytes 28311556 | tf_op jit(solution)/shard_map/while
  416.8 8.7 %copy-start.2 = (f32[3,512,1536]{2,1,0:T(8,128)}, f32[3,512,1536]{2,1,0:T(8,128)S(1)}, u32[]{:S(2)}) copy-start(f32[3,512,1536]{2,1,0:T(8,128)S(1)} %fusion.163) | copy-start | bytes 28311556 | tf_op jit(solution)/shard_map/while
  469.2 186.8 %all-reduce.16.cloned.1.call-start = ((), (), s32[]{:S(2)}) async-start(), calls=%async_computation.10 | async-start | bytes 4718592 | tf_op jit(solution)/shard_map/psum | solution.py:277
  477.4 178.5 %reduce-scatter.5.cloned.1.call-start = ((), (), s32[]{:S(2)}) async-start(), calls=%async_computation.9 | async-start | bytes 2654208 | tf_op jit(solution)/shard_map/reduce_scatter | solution.py:175
  484.3 9.6 %copy-start.21 = (f32[1,1536,3,32]{1,3,2,0:T(8,128)S(1)}, f32[1,1536,3,32]{1,3,2,0:T(8,128)}, u32[]{:S(2)}) copy-start(f32[1,1536,3,32]{1,3,2,0:T(8,128)} %copy-done.20) | copy-start | bytes 1769476
  484.3 178.8 %reduce-scatter.3.cloned.1.call-start = ((), (), s32[]{:S(2)}) async-start(), calls=%async_computation.8 | async-start | bytes 2654208 | tf_op jit(solution)/shard_map/reduce_scatter | solution.py:171
  535.8 134.9 %copy-start.1 = (bf16[192,768]{1,0:T(8,128)(2,1)S(1)}, bf16[192,768]{1,0:T(8,128)(2,1)}, u32[]{:S(2)}) copy-start(bf16[192,768]{1,0:T(8,128)(2,1)} %param.31) | copy-start | bytes 884740
  (49 other events, 203.4 us)
Sparse Core Ops, SparseCore 0:
  81.4 58.3 all-reduce.7
  175.6 54.1 all-reduce.9
  252.5 55.7 all-reduce.11
  469.3 55.7 all-reduce.13
  530.0 125.8 all-reduce.15
Sparse Core Ops, SparseCore 1:
  84.0 44.1 all-gather.2
  130.2 39.8 all-gather.4
  484.4 89.4 reduce-scatter.4
  578.4 84.6 reduce-scatter.2
where the time goes:
time: 689 us; the launch traced here: 679 us
  waiting for transfers between devices  301 us (44%)
  matrix products  153 us (22%)
  other arithmetic  97.3 us (14%)
  local copies, waits for them, and re-layouts  70.2 us (10%)
  blocking collectives  38.1 us (6%)
  between operations  18.1 us (3%)
    psum x1, waiting for transfers between devices, shards(): lax.psum((grad_w_query, grad_b_query, grad_w_key, grad_b_key, grad_w_valu...  116 us
    psum x1, waiting for transfers between devices, shards(): lax.psum(jnp.dot(attn_mix, w_out, preferred_element_type=jnp.float32).ast...  56.9 us
    psum x1, waiting for transfers between devices, shards(): lax.psum(ffn_part.astype(jnp.bfloat16), 'mp').astype(jnp.float32)  55.6 us
    psum x1, waiting for transfers between devices, shards(): lax.psum(jnp.dot(active_low, tile_down, preferred_element_type=jnp.float3...  53.6 us
    psum x1, blocking collectives, shards(): lax.psum((grad_w_query, grad_b_query, grad_w_key, grad_b_key, grad_w_valu...  38.1 us
    dot_general x6, matrix products, score_block(): jnp.einsum('qhd,khd->hqk', query_blk, keyset, preferred_element_type=jnp....  30.9 us
    dynamic_update_slice x9, local copies, waits for them, and re-layouts, shards(): lax.map(one_block, (queries[index_row].reshape(block_shape), row_seg.resh...  29.4 us
    convert_element_type x3, other arithmetic, one_block(): grad_scores = (probability * (grad_prob - delta)).astype(jnp.bfloat16)  28 us
  transfers between devices with their start and end apart: 9, of which 6 were waited for; matrix products, arithmetic and copies ran while one was open for 8% of the time, Pallas kernels for 0%

commit v1 on v0

v1 whole, which is shorter than its diff:
```python
import math

import jax
import jax.numpy as jnp
from jax import lax
from jax.experimental import pallas as pl
from jax.experimental.pallas import tpu as pltpu
from jax.sharding import PartitionSpec as P

HEAD_DIM = 64
HALF_DIM = HEAD_DIM // 2
WIDE = 128
USED = 80
MASKED = -1e30
LOG2E = math.log2(math.e)
EPS = 1e-12
BLOCK = 256
bf16 = jnp.bfloat16
f32 = jnp.float32
VMEM = pl.BlockSpec(memory_space=pltpu.VMEM)
SMEM = pl.BlockSpec(memory_space=pltpu.SMEM)


def params(mib=56):
    return pltpu.CompilerParams(vmem_limit_bytes=mib * 2**20)


def out(*shape, dtype=bf16):
    return jax.ShapeDtypeStruct(shape, dtype)


def fixed(*shape):
    return pl.BlockSpec(shape, lambda i, *_: (0,) * len(shape))


def dot(left, right, left_dim, right_dim):
    return lax.dot_general(
        left, right, (((left_dim,), (right_dim,)), ((), ())), preferred_element_type=f32
    )


def qkv_body(
    len_ref, tok_ref, wq_ref, wk_ref, wv_ref, bq_ref, bk_ref, bv_ref, freq_ref,
    qa_ref, ka_ref, va_ref, cos_ref, sin_ref,
):
    n = tok_ref.shape[0]
    heads = wq_ref.shape[0] // HEAD_DIM
    pos = lax.broadcasted_iota(jnp.int32, (1, n), 1)
    first = len_ref[0, 0]
    used = first + len_ref[0, 1]
    in0, in1 = pos < first, pos < used
    start = jnp.where(in0, 0, jnp.where(in1, first, used))
    angles = freq_ref[...] * (pos - start).astype(f32)
    cosine, sine = jnp.cos(angles), jnp.sin(angles)
    cos_ref[...] = cosine
    sin_ref[...] = sine
    segment = jnp.where(in0, 0, jnp.where(in1, 1, 2))
    row = lax.broadcasted_iota(jnp.int32, (WIDE - HEAD_DIM, n), 0)
    same = row == segment
    q_tail = jnp.where(same, 1.0, 0.0).astype(bf16)
    k_tail = jnp.where(jnp.logical_or(same, row > 2), 0.0, MASKED).astype(bf16)
    v_tail = jnp.where(row < 3, 1.0, 0.0).astype(bf16)
    tok = tok_ref[...]

    def rotated(lin, h, scale):
        a = lin[h * HEAD_DIM : h * HEAD_DIM + HALF_DIM]
        b = lin[h * HEAD_DIM + HALF_DIM : (h + 1) * HEAD_DIM]
        x, y = a * cosine - b * sine, b * cosine + a * sine
        if scale != 1.0:
            x, y = x * scale, y * scale
        return x.astype(bf16), y.astype(bf16)

    for w_ref, b_ref, to_ref, tail, scale in (
        (wq_ref, bq_ref, qa_ref, q_tail, LOG2E / math.sqrt(HEAD_DIM)),
        (wk_ref, bk_ref, ka_ref, k_tail, 1.0),
        (wv_ref, bv_ref, va_ref, v_tail, None),
    ):
        lin = dot(w_ref[...], tok, 1, 1) + b_ref[...]
        for h in range(heads):
            if scale is None:
                to_ref[h, 0:HEAD_DIM] = lin[h * HEAD_DIM : (h + 1) * HEAD_DIM].astype(bf16)
            else:
                x, y = rotated(lin, h, scale)
                to_ref[h, 0:HALF_DIM] = x
                to_ref[h, HALF_DIM:HEAD_DIM] = y
            to_ref[h, HEAD_DIM:] = tail


def project(lengths, tok, wq, wk, wv, bq, bk, bv):
    n = tok.shape[0]
    heads = wq.shape[0] // HEAD_DIM
    freq = jnp.exp(jnp.arange(HALF_DIM, dtype=f32) * (-math.log(10000.0) / HALF_DIM))
    return pl.pallas_call(
        qkv_body,
        out_shape=(
            out(heads, WIDE, n), out(heads, WIDE, n), out(heads, WIDE, n),
            out(HALF_DIM, n, dtype=f32), out(HALF_DIM, n, dtype=f32),
        ),
        in_specs=[SMEM] + [VMEM] * 8,
        out_specs=(VMEM,) * 5,
        compiler_params=params(),
    )(
        lengths, tok, wq, wk, wv,
        bq.reshape(-1, 1), bk.reshape(-1, 1), bv.reshape(-1, 1), freq.reshape(-1, 1),
    )


def attend_body(qa_ref, ka_ref, va_ref, p_ref, mix_ref, inv_ref):
    for h in range(qa_ref.shape[0]):
        scores = dot(ka_ref[h], qa_ref[h], 0, 0)
        top = jnp.max(scores, axis=0, keepdims=True)
        p = jnp.exp2(scores - top).astype(bf16)
        p_ref[h] = p
        mixed = jnp.dot(va_ref[h, 0:USED], p, preferred_element_type=f32)
        inv = 1.0 / mixed[HEAD_DIM : HEAD_DIM + 1]
        mix_ref[h * HEAD_DIM : (h + 1) * HEAD_DIM] = (mixed[0:HEAD_DIM] * inv).astype(bf16)
        inv_ref[h] = inv


def attend(qa, ka, va):
    heads, _, n = qa.shape
    return pl.pallas_call(
        attend_body,
        grid=(n // BLOCK,),
        in_specs=[
            pl.BlockSpec((heads, WIDE, BLOCK), lambda i: (0, 0, i)),
            fixed(heads, WIDE, n),
            fixed(heads, WIDE, n),
        ],
        out_specs=(
            pl.BlockSpec((heads, n, BLOCK), lambda i: (0, 0, i)),
            pl.BlockSpec((heads * HEAD_DIM, BLOCK), lambda i: (0, i)),
            pl.BlockSpec((heads, 1, BLOCK), lambda i: (0, 0, i)),
        ),
        out_shape=(out(heads, n, n), out(heads * HEAD_DIM, n), out(heads, 1, n, dtype=f32)),
        compiler_params=params(),
    )(qa, ka, va)


def attend_back_body(
    do_ref, mix_ref, inv_ref, qa_ref, ka_ref, va_ref, p_ref, cos_ref, sin_ref, cos_all, sin_all,
    dq_ref, dkv_ref, dk_acc, dv_acc,
):
    heads, _, width = qa_ref.shape
    step = pl.program_id(0)

    @pl.when(step == 0)
    def _():
        dk_acc[...] = jnp.zeros_like(dk_acc)
        dv_acc[...] = jnp.zeros_like(dv_acc)

    def turned_back(a, b, cosine, sine):
        return (a * cosine + b * sine).astype(bf16), (b * cosine - a * sine).astype(bf16)

    for h in range(heads):
        lo, mid, hi = h * HEAD_DIM, h * HEAD_DIM + HALF_DIM, (h + 1) * HEAD_DIM
        do = (do_ref[lo:hi].astype(f32) * inv_ref[h]).astype(bf16)
        delta = jnp.sum(do.astype(f32) * mix_ref[lo:hi].astype(f32), axis=0, keepdims=True)
        d1 = delta.astype(bf16).astype(f32)
        d2 = (delta - d1).astype(bf16).astype(f32)
        d3 = delta - d1 - d2
        row = lax.broadcasted_iota(jnp.int32, (USED - HEAD_DIM, width), 0)
        tail = jnp.where(row == 0, -d1, jnp.where(row == 1, -d2, jnp.where(row == 2, -d3, 0.0)))
        do_wide = jnp.concatenate([do, tail.astype(bf16)], axis=0)
        dp = dot(va_ref[h, 0:USED], do_wide, 0, 0)
        p = p_ref[h]
        ds = p * dp.astype(bf16)
        dq = jnp.dot(ka_ref[h, 0:HEAD_DIM], ds, preferred_element_type=f32)
        dq = dq * (1.0 / math.sqrt(HEAD_DIM))
        x, y = turned_back(dq[0:HALF_DIM], dq[HALF_DIM:HEAD_DIM], cos_ref[...], sin_ref[...])
        dq_ref[lo:mid] = x
        dq_ref[mid:hi] = y
        dk_acc[lo:hi] += dot(qa_ref[h, 0:HEAD_DIM], ds, 1, 1)
        dv_acc[lo:hi] += dot(do, p, 1, 1)

    @pl.when(step == pl.num_programs(0) - 1)
    def _():
        w = heads * HEAD_DIM
        for h in range(heads):
            lo, mid, hi = h * HEAD_DIM, h * HEAD_DIM + HALF_DIM, (h + 1) * HEAD_DIM
            a, b = dk_acc[lo:mid] * math.log(2.0), dk_acc[mid:hi] * math.log(2.0)
            x, y = turned_back(a, b, cos_all[...], sin_all[...])
            dkv_ref[lo:mid] = x
            dkv_ref[mid:hi] = y
        dkv_ref[w:] = dv_acc[...].astype(bf16)


def attend_back(do, mix, inv, qa, ka, va, p, cosine, sine):
    heads, _, n = qa.shape
    w = heads * HEAD_DIM
    columns = pl.BlockSpec((w, BLOCK), lambda i: (0, i))
    table = pl.BlockSpec((HALF_DIM, BLOCK), lambda i: (0, i))
    return pl.pallas_call(
        attend_back_body,
        grid=(n // BLOCK,),
        in_specs=[
            columns,
            columns,
            pl.BlockSpec((heads, 1, BLOCK), lambda i: (0, 0, i)),
            pl.BlockSpec((heads, WIDE, BLOCK), lambda i: (0, 0, i)),
            fixed(heads, WIDE, n),
            fixed(heads, WIDE, n),
            pl.BlockSpec((heads, n, BLOCK), lambda i: (0, 0, i)),
            table,
            table,
            fixed(HALF_DIM, n),
            fixed(HALF_DIM, n),
        ],
        out_specs=(columns, fixed(2 * w, n)),
        out_shape=(out(w, n), out(2 * w, n)),
        scratch_shapes=[pltpu.VMEM((w, n), f32), pltpu.VMEM((w, n), f32)],
        compiler_params=params(),
    )(do, mix, inv, qa, ka, va, p, cosine, sine, cosine, sine)


def near(shape, blocks):
    return pl.BlockSpec(shape, lambda i, *_: (jnp.minimum(i, blocks - 1), 0))


def far(shape, blocks):
    return pl.BlockSpec(shape, lambda i, *_: (jnp.maximum(i - blocks, 0), 0))


def true_block(i, where, blocks):
    return lax.rem(i + where[0] * blocks, 2 * blocks)


def forward_body(
    where_ref, order_ref, mix_a, mix_b, wo_a, wo_b, tok_ref, bo_ref, gain_ref, shift_ref,
    near_ref, far_ref, bi_ref,
    low_ref, unit_ref, scale_ref, act_ref, slope_ref, own_ref, other_ref, wi_ref, wd_ref,
):
    step = pl.program_id(0)
    half = pl.num_programs(0) // 2

    @pl.when(step == 0)
    def _():
        parts = order_ref.shape[0]
        rows = wi_ref.shape[0] // parts
        for j in range(parts):
            from_ref, k = (near_ref, j) if j < near_ref.shape[0] else (far_ref, j - near_ref.shape[0])
            at = pl.ds(pl.multiple_of(order_ref[j] * rows, rows), rows)
            wi_ref[at] = from_ref[k, 0]
            wd_ref[at] = from_ref[k, 1]

    z = tok_ref[...].astype(f32) + dot(mix_a[...], wo_a[...], 0, 0) + dot(mix_b[...], wo_b[...], 0, 0)
    z = z + bo_ref[...]
    center = z - jnp.mean(z, axis=-1, keepdims=True)
    scale = lax.rsqrt(jnp.mean(center * center, axis=-1, keepdims=True) + EPS)
    unit = center * scale
    low = (unit * gain_ref[...] + shift_ref[...]).astype(bf16)
    low_ref[...] = low
    unit_ref[...] = unit
    scale_ref[...] = scale
    inner = jnp.dot(low, wi_ref[...], preferred_element_type=f32) + bi_ref[...]
    phi = 0.5 * lax.erf(inner * math.sqrt(0.5)) + 0.5
    act = (inner * phi).astype(bf16)
    bell = jnp.exp2(inner * inner * (-0.5 * LOG2E)) * (1.0 / math.sqrt(2.0 * math.pi))
    act_ref[...] = act
    slope_ref[...] = (phi + inner * bell).astype(bf16)
    part = dot(act, wd_ref[...], 1, 1).astype(bf16)

    @pl.when(step < half)
    def _():
        own_ref[...] = part

    @pl.when(step >= half)
    def _():
        other_ref[...] = part


def feed_forward(where, order, mix_a, mix_b, wo_a, wo_b, tok, bo, gain, shift, w_near, w_far, bi):
    n, d = tok.shape
    hidden = bi.shape[1]
    blocks = n // BLOCK // 2
    w2 = mix_a.shape[0]
    columns = pl.BlockSpec((w2, BLOCK), lambda i, where, order: (0, true_block(i, where, blocks)))
    rows = pl.BlockSpec((BLOCK, d), lambda i, where, order: (i, 0))
    wide = pl.BlockSpec((BLOCK, hidden), lambda i, where, order: (i, 0))
    return pl.pallas_call(
        forward_body,
        grid_spec=pltpu.PrefetchScalarGridSpec(
            num_scalar_prefetch=2,
            grid=(2 * blocks,),
            in_specs=[
                columns, columns, fixed(w2, d), fixed(w2, d),
                pl.BlockSpec((BLOCK, d), lambda i, where, order: (true_block(i, where, blocks), 0)),
                fixed(1, d), fixed(1, d), fixed(1, d),
                fixed(*w_near.shape), fixed(*w_far.shape), fixed(1, hidden),
            ],
            out_specs=(
                rows, rows, pl.BlockSpec((BLOCK, 1), lambda i, where, order: (i, 0)), wide, wide,
                near((BLOCK, d), blocks), far((BLOCK, d), blocks),
                fixed(d, hidden), fixed(d, hidden),
            ),
        ),
        out_shape=(
            out(n, d), out(n, d, dtype=f32), out(n, 1, dtype=f32), out(n, hidden), out(n, hidden),
            out(n // 2, d), out(n // 2, d), out(d, hidden), out(d, hidden),
        ),
        compiler_params=params(),
    )(where, order, mix_a, mix_b, wo_a, wo_b, tok, bo, gain, shift, w_near, w_far, bi)


def norm_back(g, unit, scale, gain):
    q = g * gain
    return scale * (
        q - jnp.mean(q, axis=-1, keepdims=True) - unit * jnp.mean(q * unit, axis=-1, keepdims=True)
    )


def column_sums(sums_ref, *terms):
    @pl.when(pl.program_id(0) == 0)
    def _():
        sums_ref[...] = jnp.zeros_like(sums_ref)

    for k, term in enumerate(terms):
        sums_ref[k : k + 1] += jnp.sum(term, axis=0, keepdims=True)


def second_norm_body(
    where_ref, len_ref, unit_ref, gain1_ref, shift1_ref, mine_ref, theirs_ref, bd_ref, gain_ref,
    shift_ref, cot_ref, out_ref, low_ref, sums_ref,
):
    step = pl.program_id(0)
    rows = unit_ref.shape[0]
    total = mine_ref[...].astype(f32) + theirs_ref[...].astype(f32)
    z = unit_ref[...] * gain1_ref[...] + shift1_ref[...] + total + bd_ref[...]
    center = z - jnp.mean(z, axis=-1, keepdims=True)
    scale = lax.rsqrt(jnp.mean(center * center, axis=-1, keepdims=True) + EPS)
    unit = center * scale
    out_ref[...] = (unit * gain_ref[...] + shift_ref[...]).astype(bf16)
    place = (where_ref[0] * pl.num_programs(0) + step) * rows
    place = place + lax.broadcasted_iota(jnp.int32, (rows, 1), 0)
    g = jnp.where(place < len_ref[0, 0] + len_ref[0, 1], cot_ref[...], 0.0)
    back = norm_back(g, unit, scale, gain_ref[...])
    low_ref[...] = back.astype(bf16)
    column_sums(sums_ref, g * unit, g, back)


def second_norm(where, lengths, unit, gain1, shift1, mine, theirs, bd, gain, shift, cot):
    n, d = cot.shape
    blocks = n // BLOCK // 2
    rows = pl.BlockSpec((BLOCK, d), lambda i, where, lens: (i, 0))
    return pl.pallas_call(
        second_norm_body,
        grid_spec=pltpu.PrefetchScalarGridSpec(
            num_scalar_prefetch=2,
            grid=(blocks,),
            in_specs=[
                rows, fixed(1, d), fixed(1, d), rows, rows, fixed(1, d), fixed(1, d), fixed(1, d),
                pl.BlockSpec((BLOCK, d), lambda i, where, lens: (where[0] * blocks + i, 0)),
            ],
            out_specs=(rows, rows, fixed(8, d)),
        ),
        out_shape=(out(n // 2, d), out(n // 2, d), out(8, d, dtype=f32)),
        compiler_params=params(),
    )(where, lengths, unit, gain1, shift1, mine, theirs, bd, gain, shift, cot)


def first_norm_body(unit_ref, scale_ref, gain_ref, skip_ref, mine_ref, theirs_ref, low_ref, sums_ref):
    g = skip_ref[...].astype(f32) + (mine_ref[...].astype(f32) + theirs_ref[...].astype(f32))
    unit = unit_ref[...]
    back = norm_back(g, unit, scale_ref[...], gain_ref[...])
    low_ref[...] = back.astype(bf16)
    column_sums(sums_ref, g * unit, g, back)


def first_norm(unit, scale, gain, skip, mine, theirs):
    half, d = skip.shape
    rows = pl.BlockSpec((BLOCK, d), lambda i: (i, 0))
    return pl.pallas_call(
        first_norm_body,
        grid=(half // BLOCK,),
        in_specs=[rows, pl.BlockSpec((BLOCK, 1), lambda i: (i, 0)), fixed(1, d), rows, rows, rows],
        out_specs=(rows, fixed(8, d)),
        out_shape=(out(half, d), out(8, d, dtype=f32)),
        compiler_params=params(),
    )(unit, scale, gain, skip, mine, theirs)


def backward_body(near_ref, far_ref, wi_ref, wd_ref, slope_ref, gi_ref, own_ref, other_ref, sums_ref):
    step = pl.program_id(0)
    half = pl.num_programs(0) // 2

    def run(from_ref, to_ref):
        g = jnp.dot(from_ref[...], wd_ref[...], preferred_element_type=f32)
        g = (g * slope_ref[...].astype(f32)).astype(bf16)
        gi_ref[...] = g
        to_ref[...] = dot(g, wi_ref[...], 1, 1).astype(bf16)
        column_sums(sums_ref, g.astype(f32))

    @pl.when(step < half)
    def _():
        run(near_ref, own_ref)

    @pl.when(step >= half)
    def _():
        run(far_ref, other_ref)


def feed_back(low_near, low_far, wi, wd, slope):
    n, hidden = slope.shape
    half, d = low_near.shape
    blocks = half // BLOCK
    wide = pl.BlockSpec((BLOCK, hidden), lambda i: (i, 0))
    return pl.pallas_call(
        backward_body,
        grid=(2 * blocks,),
        in_specs=[
            near((BLOCK, d), blocks), far((BLOCK, d), blocks), fixed(d, hidden), fixed(d, hidden), wide,
        ],
        out_specs=(wide, near((BLOCK, d), blocks), far((BLOCK, d), blocks), fixed(8, hidden)),
        out_shape=(out(n, hidden), out(half, d), out(half, d), out(8, hidden, dtype=f32)),
        compiler_params=params(),
    )(low_near, low_far, wi, wd, slope)


def weight_grad_body(order_ref, low_ref, gi_ref, near_ref, far_ref, act_ref, *refs):
    *to_refs, grad_ref = refs
    half = near_ref.shape[0]

    def spread(which):
        first = to_refs[0].shape[0]
        rows = to_refs[0].shape[2]
        for j in range(order_ref.shape[0]):
            to_ref, k = (to_refs[0], j) if j < first else (to_refs[1], j - first)
            at = pl.ds(pl.multiple_of(order_ref[j] * rows, rows), rows)
            to_ref[k, which] = grad_ref[at].astype(bf16)

    grad_ref[...] = dot(low_ref[...], gi_ref[...], 0, 0)
    spread(0)
    grad_ref[...] = dot(near_ref[...], act_ref[0:half], 0, 0) + dot(far_ref[...], act_ref[half:], 0, 0)
    spread(1)


def weight_grads(order, low, gi, near_half, far_half, act):
    n, d = low.shape
    hidden = act.shape[1]
    width = BLOCK
    parts = order.shape[0]
    sizes = (1,) if parts == 1 else (parts // 2, parts // 2)
    rows = d // parts
    wide = pl.BlockSpec((n, width), lambda i, order: (0, i))
    return pl.pallas_call(
        weight_grad_body,
        grid_spec=pltpu.PrefetchScalarGridSpec(
            num_scalar_prefetch=1,
            grid=(hidden // width,),
            in_specs=[fixed(n, d), wide, fixed(n // 2, d), fixed(n // 2, d), wide],
            out_specs=tuple(
                pl.BlockSpec((k, 2, rows, width), lambda i, order: (0, 0, 0, i)) for k in sizes
            ),
            scratch_shapes=[pltpu.VMEM((d, width), f32)],
        ),
        out_shape=tuple(out(k, 2, rows, hidden) for k in sizes),
        compiler_params=params(),
    )(order, low, gi, near_half, far_half, act)


def mix_back_body(where_ref, near_ref, far_ref, wo_ref, mix_ref, do_ref, pick_ref, gwo_ref):
    step = pl.program_id(0)
    half = pl.num_programs(0) // 2
    w, d = wo_ref.shape

    @pl.when(step == 0)
    def _():
        gwo_ref[...] = jnp.zeros_like(gwo_ref)

    row = lax.broadcasted_iota(jnp.int32, (w, d), 0) + where_ref[1] * w
    chosen = jnp.where(row == lax.broadcasted_iota(jnp.int32, (w, d), 1), 1.0, 0.0).astype(bf16)

    def run(from_ref):
        g = from_ref[...]
        do_ref[...] = dot(wo_ref[...], g, 1, 1).astype(bf16)
        pick_ref[...] = dot(chosen, g, 1, 1).astype(bf16)
        gwo_ref[...] += jnp.dot(mix_ref[...], g, preferred_element_type=f32)

    @pl.when(step < half)
    def _():
        run(near_ref)

    @pl.when(step >= half)
    def _():
        run(far_ref)


def mix_back(where, near_half, far_half, wo, mix):
    half, d = near_half.shape
    w = wo.shape[0]
    blocks = half // BLOCK
    columns = pl.BlockSpec((w, BLOCK), lambda i, where: (0, true_block(i, where, blocks)))
    return pl.pallas_call(
        mix_back_body,
        grid_spec=pltpu.PrefetchScalarGridSpec(
            num_scalar_prefetch=1,
            grid=(2 * blocks,),
            in_specs=[near((BLOCK, d), blocks), far((BLOCK, d), blocks), fixed(w, d), columns],
            out_specs=(columns, columns, fixed(w, d)),
        ),
        out_shape=(out(w, 2 * half), out(w, 2 * half), out(w, d, dtype=f32)),
        compiler_params=params(),
    )(where, near_half, far_half, wo, mix)


def project_grad_body(order_ref, dq_ref, dkv_ref, tok_ref, gwo_ref, bias_ref, *refs):
    *to_refs, grad_ref = refs
    w = dq_ref.shape[0]
    tok = tok_ref[...]
    grad_ref[0:w] = jnp.dot(dq_ref[...], tok, preferred_element_type=f32)
    grad_ref[w : 3 * w] = jnp.dot(dkv_ref[...], tok, preferred_element_type=f32)
    grad_ref[3 * w :] = gwo_ref[...]
    bias_ref[0:w] = jnp.sum(dq_ref[...].astype(f32), axis=1, keepdims=True)
    bias_ref[w:] = jnp.sum(dkv_ref[...].astype(f32), axis=1, keepdims=True)
    first = to_refs[0].shape[0]
    rows = to_refs[0].shape[1]
    for j in range(order_ref.shape[0]):
        to_ref, k = (to_refs[0], j) if j < first else (to_refs[1], j - first)
        at = pl.ds(pl.multiple_of(order_ref[j] * rows, rows), rows)
        to_ref[k] = grad_ref[at].astype(bf16)


def project_grads(order, dq, dkv, tok, gwo):
    w, n = dq.shape
    d = tok.shape[1]
    parts = order.shape[0]
    sizes = (1,) if parts == 1 else (parts // 2, parts // 2)
    return pl.pallas_call(
        project_grad_body,
        in_specs=[SMEM] + [VMEM] * 4,
        out_specs=(VMEM,) * (1 + len(sizes)),
        out_shape=(out(3 * w, 1, dtype=f32),) + tuple(out(k, 4 * w // parts, d) for k in sizes),
        scratch_shapes=[pltpu.VMEM((4 * w, d), f32)],
        compiler_params=params(),
    )(order, dq, dkv, tok, gwo)


def input_grad_body(share_ref, dq_ref, dkv_ref, wq_ref, wk_ref, wv_ref, here_ref, there_ref, all_ref):
    w = dq_ref.shape[0]
    part = dot(wq_ref[...], dq_ref[...], 0, 0)
    part = part + dot(wk_ref[...], dkv_ref[0:w], 0, 0)
    all_ref[...] = part + dot(wv_ref[...], dkv_ref[w:], 0, 0)
    for j in range(4):
        at = pl.ds(pl.multiple_of(share_ref[j] * w, w), w)
        to_ref = here_ref if j < 2 else there_ref
        to_ref[j % 2] = all_ref[at].astype(bf16)


def input_grads(shares, dq, dkv, wq, wk, wv):
    w, n = dq.shape
    d = wq.shape[1]
    width = 2 * BLOCK
    split = pl.BlockSpec((2, w, width), lambda i, shares: (0, 0, i))
    return pl.pallas_call(
        input_grad_body,
        grid_spec=pltpu.PrefetchScalarGridSpec(
            num_scalar_prefetch=1,
            grid=(n // width,),
            in_specs=[
                pl.BlockSpec((w, width), lambda i, shares: (0, i)),
                pl.BlockSpec((2 * w, width), lambda i, shares: (0, i)),
                fixed(w, d), fixed(w, d), fixed(w, d),
            ],
            out_specs=(split, split),
            scratch_shapes=[pltpu.VMEM((d, width), f32)],
        ),
        out_shape=(out(2, w, n), out(2, w, n)),
        compiler_params=params(),
    )(shares, dq, dkv, wq, wk, wv)


def settle_body(order_ref, near_ref, far_ref, q_ref, k_ref, v_ref, o_ref, all_ref):
    rows = near_ref.shape[1]
    first = near_ref.shape[0]
    for j in range(order_ref.shape[0]):
        from_ref, k = (near_ref, j) if j < first else (far_ref, j - first)
        at = pl.ds(pl.multiple_of(order_ref[j] * rows, rows), rows)
        all_ref[at] = from_ref[k].astype(f32)
    w = q_ref.shape[0]
    for k, to_ref in enumerate((q_ref, k_ref, v_ref, o_ref)):
        to_ref[...] = all_ref[k * w : (k + 1) * w]


def settle(order, near_part, far_part, w):
    d = near_part.shape[-1]
    return pl.pallas_call(
        settle_body,
        in_specs=[SMEM] + [VMEM] * 2,
        out_specs=(VMEM,) * 4,
        out_shape=(out(w, d, dtype=f32),) * 4,
        scratch_shapes=[pltpu.VMEM((4 * w, d), f32)],
        compiler_params=params(),
    )(order, near_part, far_part)


def halves_body(where_ref, near_ref, far_ref, to_ref):
    mine = pl.program_id(0) // (pl.num_programs(0) // 2) == where_ref[0]

    @pl.when(mine)
    def _():
        to_ref[...] = near_ref[...]

    @pl.when(jnp.logical_not(mine))
    def _():
        to_ref[...] = far_ref[...]


def halves(where, near_half, far_half):
    half, d = near_half.shape
    rows = half // 2
    take = pl.BlockSpec((rows, d), lambda i, where: (lax.rem(i, 2), 0))
    return pl.pallas_call(
        halves_body,
        grid_spec=pltpu.PrefetchScalarGridSpec(
            num_scalar_prefetch=1,
            grid=(4,),
            in_specs=[take, take],
            out_specs=pl.BlockSpec((rows, d), lambda i, where: (i, 0)),
        ),
        out_shape=out(2 * half, d),
        compiler_params=params(),
    )(where, near_half, far_half)


def swap(x, axis, bit):
    return lax.ppermute(x, axis, [(i, i ^ bit) for i in range(lax.axis_size(axis))])


def add_low(a, b):
    return (a.astype(f32) + b.astype(f32)).astype(bf16)


def shards(
    tokens, lengths, w_query, b_query, w_key, b_key, w_value, b_value, w_out, b_out, ln1_gain,
    ln1_bias, w_in, b_in, w_down, b_down, ln2_gain, ln2_bias, cotangent,
):
    dp = lax.axis_size("dp")
    n, d = tokens.shape
    w = w_query.shape[1]
    line = lambda v: v.reshape(1, -1)
    me = lax.axis_index("mp")
    core = me % 2
    where = jnp.stack([core, me]).astype(jnp.int32)
    wq, wk, wv = w_query.T, w_key.T, w_value.T

    stepwise = dp & (dp - 1) == 0 and dp > 1 and (d // dp) % 16 == 0
    bits = [1 << k for k in range(dp.bit_length() - 1)] if stepwise else []
    parts = 1 << len(bits)
    order = jnp.zeros((1,), jnp.int32)
    if stepwise:
        count = len(bits)
        places = [
            sum(bit for k, bit in enumerate(bits) if j >> (count - 1 - k) & 1) for j in range(parts)
        ]
        order = lax.axis_index("dp") ^ jnp.array(places, jnp.int32)

    def gather(own):
        held = own
        for bit in reversed(bits[1:]):
            held = jnp.concatenate([held, swap(held, "dp", bit)], axis=0)
        return held, swap(held, "dp", bits[0])

    def scatter_sum(keep, send):
        for k, bit in enumerate(bits):
            total = add_low(keep, swap(send, "dp", bit)) if k + 1 < len(bits) else (
                keep.astype(f32) + swap(send, "dp", bit).astype(f32)
            )
            keep, send = jnp.split(total, 2, axis=0) if k + 1 < len(bits) else (total, None)
        return keep

    if stepwise:
        w_near, w_far = gather(jnp.stack([w_in, w_down.T])[None])
    else:
        w_near = jnp.stack([
            lax.all_gather(w_in, "dp", axis=0, tiled=True),
            lax.all_gather(w_down.T, "dp", axis=0, tiled=True),
        ])[None]
        w_far = jnp.zeros((1, 2, 16, w_near.shape[-1]), bf16)
    wo_a = jnp.concatenate([w_out, swap(w_out, "mp", 2)], axis=0)
    wo_b = swap(wo_a, "mp", 1)

    qa, ka, va, cosine, sine = project(lengths, tokens, wq, wk, wv, b_query, b_key, b_value)
    p, mix, inv = attend(qa, ka, va)
    mix_a = jnp.concatenate([mix, swap(mix, "mp", 2)], axis=0)
    mix_b = swap(mix_a, "mp", 1)
    low, unit, scale, act, slope, own, other, wi, wd = feed_forward(
        where, order, mix_a, mix_b, wo_a, wo_b, tokens, line(b_out), line(ln1_gain), line(ln1_bias),
        w_near, w_far, line(b_in),
    )
    mine = add_low(own, swap(other, "mp", 1))
    theirs = swap(mine, "mp", 2)
    half_out, result_near, sums_two = second_norm(
        where, lengths, unit, line(ln1_gain), line(ln1_bias), mine, theirs, line(b_down),
        line(ln2_gain), line(ln2_bias), cotangent,
    )
    result_far = swap(result_near, "mp", 1)
    layer_out = halves(where, half_out, swap(half_out, "mp", 1))

    gi, own, other, sums_in = feed_back(result_near, result_far, wi, wd, slope)
    mine = add_low(own, swap(other, "mp", 1))
    theirs = swap(mine, "mp", 2)
    grads = weight_grads(order, low, gi, result_near, result_far, act)
    if stepwise:
        grads = scatter_sum(*grads)[0]
        grad_w_in, grad_w_down = grads[0], grads[1]
    else:
        grad_w_in, grad_w_down = (
            lax.psum_scatter(grads[0][0, k].astype(f32), "dp", scatter_dimension=0, tiled=True)
            for k in range(2)
        )
    near_half, sums_one = first_norm(unit, scale, line(ln1_gain), result_near, mine, theirs)
    far_half = swap(near_half, "mp", 1)
    do, pick, gwo = mix_back(where, near_half, far_half, w_out, mix)
    dq, dkv = attend_back(do, mix, inv, qa, ka, va, p, cosine, sine)

    shares = me ^ jnp.array([0, 2, 1, 3], jnp.int32)
    here, there = input_grads(shares, dq, dkv, wq, wk, wv)
    sum_here = here.astype(f32) + swap(there, "mp", 1).astype(f32)
    last = swap(sum_here[1].astype(bf16), "mp", 2)
    grad_tokens = sum_here[0] + last.astype(f32) + pick.astype(f32)

    bias, *pieces = project_grads(order, dq, dkv, tokens, gwo)
    norm_sums = jnp.concatenate([sums_one[0:3], sums_two[0:3]], axis=0)
    norm_sums = norm_sums + swap(norm_sums, "mp", 1)
    sums = jnp.concatenate([norm_sums, sums_in[0:1], jnp.pad(bias.reshape(1, -1), ((0, 0), (0, d - 3 * w)))])
    if stepwise:
        mine = scatter_sum(*pieces).astype(bf16)
        near_part, far_part = gather(mine)
        for bit in bits:
            sums = sums + swap(sums, "dp", bit)
    else:
        near_part = lax.psum(pieces[0].astype(f32), "dp").astype(bf16)
        far_part = jnp.zeros((1, 16, d), bf16)
        sums = lax.psum(sums, "dp")
    gq, gk, gv, go = settle(order, near_part, far_part, w)
    g1, s1, bo, g2, s2, bd, bi, qkv = (sums[k] for k in range(8))
    return (
        layer_out, grad_tokens.T, gq.T, qkv[0:w], gk.T, qkv[w : 2 * w], gv.T, qkv[2 * w : 3 * w],
        go, bo, g1, s1, grad_w_in, bi, grad_w_down.T, bd, g2, s2,
    )


def solution(mesh):
    in_specs = (
        P("dp", None), P("dp", None),
        P(None, "mp"), P("mp"), P(None, "mp"), P("mp"), P(None, "mp"), P("mp"),
        P("mp", None), P(), P(), P(),
        P("dp", "mp"), P("mp"), P("mp", "dp"), P(), P(), P(),
        P("dp", None),
    )
    out_specs = (
        P("dp", None), P("dp", "mp"),
        P(None, "mp"), P("mp"), P(None, "mp"), P("mp"), P(None, "mp"), P("mp"),
        P("mp", None), P(), P(), P(),
        P("dp", "mp"), P("mp"), P("mp", "dp"), P(), P(), P(),
    )
    return jax.shard_map(shards, mesh=mesh, in_specs=in_specs, out_specs=out_specs, check_vma=False)
```

time: 689 us -> 310 us (0.45)
  waiting for transfers between devices: 301 us -> 119 us
  matrix products: 153 us -> 0 us
  Pallas kernels: 0 us -> 129 us
  other arithmetic: 97.3 us -> 9.86 us
  local copies, waits for them, and re-layouts: 70.2 us -> 18 us
  blocking collectives: 38.1 us -> 0 us
  starting transfers between devices: 1.15 us -> 29.4 us
  between operations: 18.1 us -> 1.16 us
    psum x5 -> x0, waiting for transfers between devices: 282 us -> none  [the longest x1 116 us: shards(): lax.psum((grad_w_query, grad_b_query, grad_w_key, grad_b_key, grad_w_valu...]
    dot_general x39 -> x0, matrix products: 153 us -> none  [the longest x6 30.9 us: score_block(): jnp.einsum('qhd,khd->hqk', query_blk, keyset, preferred_element_type=jnp....]
    pallas_call x0 -> x13, Pallas kernels: none -> 129 us  [the longest x1 25 us: attend_back(): pl.pallas_call(attend_back_body, grid=(n // BLOCK,), in_specs=[columns, c...]
    ppermute x0 -> x29, waiting for transfers between devices: none -> 119 us  [swap(): lax.ppermute(x, axis, [(i, i ^ bit) for i in range(lax.axis_size(axis))])]
    reduce_sum x15 -> x0, other arithmetic: 40.4 us -> none  [the longest x3 14.1 us: layer_norm(): return center * lax.rsqrt(spread + norm_eps) * gain_vec + shift_vec]
    psum x1 -> x0, blocking collectives: 38.1 us -> none  [shards(): lax.psum((grad_w_query, grad_b_query, grad_w_key, grad_b_key, grad_w_valu...]
    convert_element_type x8 -> x7, other arithmetic: 33.9 us -> 3.86 us  [the longest x6 3.83 us: add_low(): return (a.astype(f32) + b.astype(f32)).astype(bf16)]
    dynamic_update_slice x9 -> x0, local copies, waits for them, and re-layouts: 29.4 us -> none  [shards(): lax.map(one_block, (queries[index_row].reshape(block_shape), row_seg.resh...]
  transfers between devices with their start and end apart: 9 -> 29, of which waited for: 6 -> 17; matrix products, arithmetic and copies ran while one was open for 8% -> 6% of each run, Pallas kernels for 0% -> 30%
where the time goes in v1:
time: 310 us; the launch traced here: 306 us
  Pallas kernels  129 us (42%)
  waiting for transfers between devices  119 us (38%)
  starting transfers between devices  29.4 us (9%)
  local copies, waits for them, and re-layouts  18 us (6%)
  other arithmetic  9.86 us (3%)
    ppermute x29, waiting for transfers between devices, swap(): lax.ppermute(x, axis, [(i, i ^ bit) for i in range(lax.axis_size(axis))])  119 us
    ppermute x29, starting transfers between devices, swap(): lax.ppermute(x, axis, [(i, i ^ bit) for i in range(lax.axis_size(axis))])  29.4 us
    pallas_call x1, Pallas kernels, attend_back(): pl.pallas_call(attend_back_body, grid=(n // BLOCK,), in_specs=[columns, c...  25 us
    pallas_call x1, Pallas kernels, attend(): pl.pallas_call(attend_body, grid=(n // BLOCK,), in_specs=[pl.BlockSpec((h...  21 us
    pallas_call x1, Pallas kernels, feed_forward(): pl.pallas_call(forward_body, grid_spec=pltpu.PrefetchScalarGridSpec(num_s...  19 us
    pallas_call x1, Pallas kernels, feed_back(): pl.pallas_call(backward_body, grid=(2 * blocks,), in_specs=[near((BLOCK,...  9.91 us
    pallas_call x1, Pallas kernels, weight_grads(): pl.pallas_call(weight_grad_body, grid_spec=pltpu.PrefetchScalarGridSpec(n...  9.14 us
    pallas_call x1, Pallas kernels, mix_back(): pl.pallas_call(mix_back_body, grid_spec=pltpu.PrefetchScalarGridSpec(num_...  7.65 us
  transfers between devices with their start and end apart: 29, of which 17 were waited for; matrix products, arithmetic and copies ran while one was open for 6% of the time, Pallas kernels for 30%

profile of v1, /device:TPU:0, one launch (start us, length us, event | category | flops | bytes accessed | tf_op | source)
XLA Modules:
  0.0 306.1 jit_solution(17182471308258024160)
XLA Ops:
  1.7 4.1 %collective-permute-start.4 = (bf16[1,2,96,768]{3,2,1,0:T(8,128)(2,1)S(1)}, bf16[1,2,96,768]{3,2,1,0:T(8,128)(2,1)S(1)}, u32[]{:S(2)}, u32[]{:S(2)}) collective-permute-start(bf16[1,2,96,768]{3,2,1,0:T(8,128)(2,1)S(1)} %maximum_bitcast_fusion), channel_id=1, source_target_pairs={{0,16},{4,20},{8,24},{12,28},{16,0},{20,4},{24,8},{28,12},{1,17},{... | collective-permute-start | bytes 884744 | tf_op jit(solution)/shard_map/ppermute | solution.py:626
  10.7 6.1 %shard_map.340 = (bf16[3,128,1536]{2,1,0:T(8,128)(2,1)}, bf16[3,128,1536]{2,1,0:T(8,128)(2,1)}, bf16[3,128,1536]{2,1,0:T(8,128)(2,1)}, f32[32,1536]{1,0:T(8,128)}, f32[32,1536]{1,0:T(8,128)}) custom-call(s32[1,2]{1,0:T(1,128)} %len_ref.3, bf16[1536,768]{1,0:T(8,128)(2,1)} %tok_ref.5, bf16[192,768]{1,0:T(8,128)(2,1)} %bitcast.38, bf16[192,768]{1,0:T(8,128)(2,1)} %bitcast.40, ...), custom_call_target="tpu_custom_call" | custom-call | tf_op jit(solution)/shard_map/pallas_call | solution.py:93
  16.8 21.0 %shard_map.341 = (bf16[3,1536,1536]{2,1,0:T(8,128)(2,1)}, bf16[192,1536]{1,0:T(8,128)(2,1)}, f32[3,1,1536]{2,1,0:T(1,128)}) custom-call(bf16[3,128,1536]{2,1,0:T(8,128)(2,1)} %get-tuple-element.60.qa_ref, bf16[3,128,1536]{2,1,0:T(8,128)(2,1)} %get-tuple-element.61.ka_ref, bf16[3,128,1536]{2,1,0:T(8,128)(2,1)} %get-tuple-element.62.va_ref), custom_call_target="tpu_custom_call" | custom-call | tf_op jit(solution)/shard_map/pallas_call | solution.py:122
  41.2 11.7 %collective-permute-done = bf16[192,1536]{1,0:T(8,128)(2,1)S(1)} collective-permute-done((bf16[192,1536]{1,0:T(8,128)(2,1)}, bf16[192,1536]{1,0:T(8,128)(2,1)S(1)}, u32[]{:S(2)}, u32[]{:S(2)}) %collective-permute-start) | collective-permute-done | bytes 589856 | tf_op jit(solution)/shard_map/ppermute | solution.py:626
  56.3 7.6 %collective-permute-done.2 = bf16[192,768]{1,0:T(8,128)(2,1)S(1)} collective-permute-done((bf16[192,768]{1,0:T(8,128)(2,1)S(1)}, bf16[192,768]{1,0:T(8,128)(2,1)S(1)}, u32[]{:S(2)}, u32[]{:S(2)}) %collective-permute-start.2) | collective-permute-done | bytes 294944 | tf_op jit(solution)/shard_map/ppermute | solution.py:626
  68.2 13.5 %collective-permute-done.6.far_ref = bf16[4,2,96,768]{3,2,1,0:T(8,128)(2,1)} collective-permute-done((bf16[4,2,96,768]{3,2,1,0:T(8,128)(2,1)S(1)}, bf16[4,2,96,768]{3,2,1,0:T(8,128)(2,1)}, u32[]{:S(2)}, u32[]{:S(2)}) %collective-permute-start.6) | collective-permute-done | bytes 1179680 | tf_op jit(solution)/shard_map/ppermute | solution.py:626
  81.8 19.0 %shard_map.342 = (bf16[1536,768]{1,0:T(8,128)(2,1)}, f32[1536,768]{1,0:T(8,128)}, f32[1536,1]{1,0:T(8,128)}, bf16[1536,768]{1,0:T(8,128)(2,1)}, bf16[1536,768]{1...) custom-call(s32[2]{0:T(128)} %pad_add_fusion.where_ref, ...), custom_call_target="tpu_custom_call" | custom-call | tf_op jit(solution)/shard_map/pallas_call | solution.py:280
  100.8 3.0 collective-permute-done.7
  108.8 24.7 %collective-permute-done.8.theirs_ref = bf16[768,768]{1,0:T(8,128)(2,1)S(1)} collective-permute-done((bf16[768,768]{1,0:T(8,128)(2,1)S(1)}, bf16[768,768]{1,0:T(8,128)(2,1)S(1)}, u32[]{:S(2)}, u32[]{:S(2)}) %collective-permute-start.8) | collective-permute-done | bytes 1179680 | tf_op jit(solution)/shard_map/ppermute | solution.py:626
  134.7 6.8 %shard_map.343 = (bf16[768,768]{1,0:T(8,128)(2,1)}, bf16[768,768]{1,0:T(8,128)(2,1)}, f32[8,768]{1,0:T(8,128)}) custom-call(s32[2]{0:T(128)} %pad_add_fusion.where_ref, s32[1,2]{1,0:T(1,128)} %len_ref.3, f32[1536,768]{1,0:T(8,128)} %get-tuple-element.64.unit_ref, f32[1,768]{1,0:T(1,128)} %reshape.95.gain_ref.gain1_ref, ...), custom_call_target="tpu_custom_call" | custom-call | tf_op jit(solution)/shard_map/pallas_call | solution.py:345
  141.5 3.0 collective-permute-done.10.far_ref
  145.6 9.9 %shard_map.345 = (bf16[1536,768]{1,0:T(8,128)(2,1)}, bf16[768,768]{1,0:T(8,128)(2,1)}, bf16[768,768]{1,0:T(8,128)(2,1)}, f32[8,768]{1,0:T(8,128)}) custom-call(bf16[768,768]{1,0:T(8,128)(2,1)} %get-tuple-element.69.near_ref.skip_ref, bf16[768,768]{1,0:T(8,128)(2,1)} %copy-done.1, bf16[768,768]{1,0:T(8,128)(2,1)} %get-tuple-element.70.wi_ref, ...), custom_call_target="tpu_custom_call" | custom-call | tf_op jit(solution)/shard_map/pallas_call | solution.py:407
  155.6 2.9 collective-permute-done.11
  161.8 9.1 %shard_map.352 = (bf16[4,2,96,768]{3,2,1,0:T(8,128)(2,1)}, bf16[4,2,96,768]{3,2,1,0:T(8,128)(2,1)}) custom-call(s32[8]{0:T(128)} %broadcast_xor_fusion.1.order_ref, bf16[1536,768]{1,0:T(8,128)(2,1)} %get-tuple-element.97.low_ref, bf16[1536,768]{1,0:T(8,128)(2,1)} %get-tuple-element.98.gi_ref, bf16[768,768]{1,0:T(8,128)(2,1)} %get-tuple-element.69.near_ref.skip_ref, ...), custom_call_target="tpu_custom_call" | custom-call | tf_op jit(solution)/shard_map/pallas_call | solution.py:445
  172.4 15.8 %collective-permute-done.12.theirs_ref = bf16[768,768]{1,0:T(8,128)(2,1)S(1)} collective-permute-done((bf16[768,768]{1,0:T(8,128)(2,1)S(1)}, bf16[768,768]{1,0:T(8,128)(2,1)S(1)}, u32[]{:S(2)}, u32[]{:S(2)}) %collective-permute-start.12) | collective-permute-done | bytes 1179680 | tf_op jit(solution)/shard_map/ppermute | solution.py:626
  189.3 5.3 %shard_map.346 = (bf16[768,768]{1,0:T(8,128)(2,1)}, f32[8,768]{1,0:T(8,128)}) custom-call(f32[1536,768]{1,0:T(8,128)} %get-tuple-element.64.unit_ref, f32[1536,1]{1,0:T(8,128)} %get-tuple-element.68.scale_ref, f32[1,768]{1,0:T(1,128)} %reshape.95.gain_ref.gain1_ref, bf16[768,768]{1,0:T(8,128)(2,1)} %get-tuple-element.69.near_ref.skip_ref, ...), custom_call_target="tpu_custom_call" | custom-call | tf_op jit(solution)/shard_map/pallas_call | solution.py:372
  195.1 3.8 %collective-permute-done.26 = bf16[4,2,96,768]{3,2,1,0:T(8,128)(2,1)S(1)} collective-permute-done((bf16[4,2,96,768]{3,2,1,0:T(8,128)(2,1)}, bf16[4,2,96,768]{3,2,1,0:T(8,128)(2,1)S(1)}, u32[]{:S(2)}, u32[]{:S(2)}) %collective-permute-start.26) | collective-permute-done | bytes 1179680 | tf_op jit(solution)/shard_map/ppermute | solution.py:626
  201.9 7.7 %shard_map.347 = (bf16[192,1536]{1,0:T(8,128)(2,1)}, bf16[192,1536]{1,0:T(8,128)(2,1)}, f32[192,768]{1,0:T(8,128)}) custom-call(s32[2]{0:T(128)} %pad_add_fusion.where_ref, bf16[768,768]{1,0:T(8,128)(2,1)} %get-tuple-element.75.near_ref, bf16[768,768]{1,0:T(8,128)(2,1)} %copy-done.12, bf16[192,768]{1,0:T(8,128)(2,1)} %wo_ref.1, ...), custom_call_target="tpu_custom_call" | custom-call | tf_op jit(solution)/shard_map/pallas_call | solution.py:493
  209.5 25.0 %shard_map.348 = (bf16[192,1536]{1,0:T(8,128)(2,1)}, bf16[384,1536]{1,0:T(8,128)(2,1)}) custom-call(bf16[192,1536]{1,0:T(8,128)(2,1)} %get-tuple-element.76.do_ref, bf16[192,1536]{1,0:T(8,128)(2,1)} %get-tuple-element.63.mix_ref, f32[3,1,1536]{2,1,0:T(1,128)} %get-tuple-element.77.inv_ref, bf16[3,128,1536]{2,1,0:T(8,128)(2,1)} %get-tuple-element.60.qa_ref, ...), custom_call_target="tpu_custom_call" | custom-call | tf_op jit(solution)/shard_map/pallas_call | solution.py:193
  234.6 5.1 %shard_map.350 = (f32[576,1]{1,0:T(8,128)}, bf16[4,96,768]{2,1,0:T(8,128)(2,1)}, bf16[4,96,768]{2,1,0:T(8,128)(2,1)}) custom-call(s32[8]{0:T(128)} %broadcast_xor_fusion.1.order_ref, bf16[192,1536]{1,0:T(8,128)(2,1)} %get-tuple-element.81.dq_ref, bf16[384,1536]{1,0:T(8,128)(2,1)} %get-tuple-element.82.dkv_ref, bf16[1536,768]{1,0:T(8,128)(2,1)} %tok_ref.5, ...), custom_call_target="tpu_custom_call" | custom-call | tf_op jit(solution)/shard_map/pallas_call | solution.py:528
  243.4 4.9 %shard_map.344 = bf16[1536,768]{1,0:T(8,128)(2,1)} custom-call(s32[2]{0:T(128)} %pad_add_fusion.where_ref, bf16[768,768]{1,0:T(8,128)(2,1)} %get-tuple-element.67.near_ref, bf16[768,768]{1,0:T(8,128)(2,1)} %copy-done.10), custom_call_target="tpu_custom_call" | custom-call | tf_op jit(solution)/shard_map/pallas_call | solution.py:612
  249.2 4.6 %collective-permute-done.16 = bf16[4,96,768]{2,1,0:T(8,128)(2,1)S(1)} collective-permute-done((bf16[4,96,768]{2,1,0:T(8,128)(2,1)}, bf16[4,96,768]{2,1,0:T(8,128)(2,1)S(1)}, u32[]{:S(2)}, u32[]{:S(2)}) %collective-permute-start.16) | collective-permute-done | bytes 589856 | tf_op jit(solution)/shard_map/ppermute | solution.py:626
  255.0 6.2 %shard_map.349 = (bf16[2,192,1536]{2,1,0:T(8,128)(2,1)}, bf16[2,192,1536]{2,1,0:T(8,128)(2,1)}) custom-call(s32[4]{0:T(128)} %broadcast_xor_fusion.share_ref, bf16[192,1536]{1,0:T(8,128)(2,1)} %get-tuple-element.81.dq_ref, bf16[384,1536]{1,0:T(8,128)(2,1)} %get-tuple-element.82.dkv_ref, bf16[192,768]{1,0:T(8,128)(2,1)} %bitcast.39, ...), custom_call_target="tpu_custom_call" | custom-call | tf_op jit(solution)/shard_map/pallas_call | solution.py:554
  262.7 4.2 %collective-permute-done.17 = bf16[2,96,768]{2,1,0:T(8,128)(2,1)S(1)} collective-permute-done((bf16[2,96,768]{2,1,0:T(8,128)(2,1)S(1)}, bf16[2,96,768]{2,1,0:T(8,128)(2,1)S(1)}, u32[]{:S(2)}, u32[]{:S(2)}) %collective-permute-start.17) | collective-permute-done | bytes 294944 | tf_op jit(solution)/shard_map/ppermute | solution.py:626
  267.6 8.4 %collective-permute-done.18 = bf16[1,96,768]{2,1,0:T(8,128)(2,1)S(1)} collective-permute-done((bf16[1,96,768]{2,1,0:T(8,128)(2,1)S(1)}, bf16[1,96,768]{2,1,0:T(8,128)(2,1)S(1)}, u32[]{:S(2)}, u32[]{:S(2)}) %collective-permute-start.18) | collective-permute-done | bytes 147488 | tf_op jit(solution)/shard_map/ppermute | solution.py:626
  276.2 3.0 collective-permute-start.25
  279.2 3.0 collective-permute-done.19
  282.7 3.2 %collective-permute-start.15 = (bf16[192,1536]{1,0:T(8,128)(2,1)S(1)}, bf16[192,1536]{1,0:T(8,128)(2,1)S(1)}, u32[]{:S(2)}, u32[]{:S(2)}) collective-permute-start(bf16[192,1536]{1,0:T(8,128)(2,1)S(1)} %fusion.3), channel_id=1, source_target_pairs={{0,2},{1,3},{2,0},{3,1},{4,6},{5,7},{6,4},{7,5},{8,10},{9,11},{10,... | collective-permute-start | bytes 1769480 | tf_op jit(solution)/shard_map/ppermute | solution.py:626
  289.0 1.7 collective-permute-start.21
  291.4 7.9 %collective-permute-done.15 = bf16[192,1536]{1,0:T(8,128)(2,1)S(1)} collective-permute-done((bf16[192,1536]{1,0:T(8,128)(2,1)S(1)}, bf16[192,1536]{1,0:T(8,128)(2,1)S(1)}, u32[]{:S(2)}, u32[]{:S(2)}) %collective-permute-start.15) | collective-permute-done | bytes 589856 | tf_op jit(solution)/shard_map/ppermute | solution.py:626
  300.5 1.9 collective-permute-done.21.far_ref
  303.2 2.8 shard_map.351
  (153 shorter events, 48.0 us)
Async XLA Ops:
  1.7 37.7 %collective-permute-start.4 = (bf16[1,2,96,768]{3,2,1,0:T(8,128)(2,1)S(1)}, bf16[1,2,96,768]{3,2,1,0:T(8,128)(2,1)S(1)}, u32[]{:S(2)}, u32[]{:S(2)}) collective-permute-start(bf16[1,2,96,768]{3,2,1,0:T(8,128)(2,1)S(1)} %maximum_bitcast_fusion), channel_id=1, source_target_pairs={{0,16},{4,20},{8,24},{12,28},{16,0},{20,4},{24,8},{28,12},{1,17},{... | collective-permute-start | bytes 884744 | tf_op jit(solution)/shard_map/ppermute | solution.py:626
  37.8 15.1 %collective-permute-start = (bf16[192,1536]{1,0:T(8,128)(2,1)}, bf16[192,1536]{1,0:T(8,128)(2,1)S(1)}, u32[]{:S(2)}, u32[]{:S(2)}) collective-permute-start(bf16[192,1536]{1,0:T(8,128)(2,1)} %get-tuple-element.63.mix_ref), channel_id=1, source_target_pairs={{0,2},{1,3},{2,0},{3,1},{4,6},{5,7},{6,4},{7,5},{8,10},{9,11},{10,... | collective-permute-start | bytes 1769480 | tf_op jit(solution)/shard_map/ppermute | solution.py:626
  39.5 14.6 %collective-permute-start.5 = (bf16[2,2,96,768]{3,2,1,0:T(8,128)(2,1)S(1)}, bf16[2,2,96,768]{3,2,1,0:T(8,128)(2,1)S(1)}, u32[]{:S(2)}, u32[]{:S(2)}) collective-permute-start(bf16[2,2,96,768]{3,2,1,0:T(8,128)(2,1)S(1)} %pad_maximum_fusion.1), channel_id=1, source_target_pairs={{0,8},{4,12},{8,0},{12,4},{16,24},{20,28},{24,16},{28,20},{1,9},{5... | collective-permute-start | bytes 1769480 | tf_op jit(solution)/shard_map/ppermute | solution.py:626
  53.0 15.3 %collective-permute-start.1 = (bf16[384,1536]{1,0:T(8,128)(2,1)S(1)}, bf16[384,1536]{1,0:T(8,128)(2,1)}, u32[]{:S(2)}, u32[]{:S(2)}) collective-permute-start(bf16[384,1536]{1,0:T(8,128)(2,1)S(1)} %constant_dynamic-update-slice_fusion.mix_a), channel_id=1, source_target_pairs={{0,1},{1,0},{2,3},{3,2},{4,5},{5,4},{6,7},{7,6},{8,9},{9,8},{10,11... | collective-permute-start | bytes 3538952 | tf_op jit(solution)/shard_map/ppermute | solution.py:626
  54.2 27.6 %copy-start.3 = (bf16[4,2,96,768]{3,2,1,0:T(8,128)(2,1)}, bf16[4,2,96,768]{3,2,1,0:T(8,128)(2,1)S(1)}, u32[]{:S(2)}) copy-start(bf16[4,2,96,768]{3,2,1,0:T(8,128)(2,1)S(1)} %pad_maximum_fusion.near_ref) | copy-start | bytes 3538948
  54.2 27.5 %collective-permute-start.6 = (bf16[4,2,96,768]{3,2,1,0:T(8,128)(2,1)S(1)}, bf16[4,2,96,768]{3,2,1,0:T(8,128)(2,1)}, u32[]{:S(2)}, u32[]{:S(2)}) collective-permute-start(bf16[4,2,96,768]{3,2,1,0:T(8,128)(2,1)S(1)} %pad_maximum_fusion.near_ref), channel_id=1, source_target_pairs={{0,4},{4,0},{8,12},{12,8},{16,20},{20,16},{24,28},{28,24},{1,5},{5... | collective-permute-start | bytes 3538952 | tf_op jit(solution)/shard_map/ppermute | solution.py:626
  55.8 8.1 %collective-permute-start.2 = (bf16[192,768]{1,0:T(8,128)(2,1)S(1)}, bf16[192,768]{1,0:T(8,128)(2,1)S(1)}, u32[]{:S(2)}, u32[]{:S(2)}) collective-permute-start(bf16[192,768]{1,0:T(8,128)(2,1)S(1)} %copy-done.13), channel_id=1, source_target_pairs={{0,2},{1,3},{2,0},{3,1},{4,6},{5,7},{6,4},{7,5},{8,10},{9,11},{10,... | collective-permute-start | bytes 884744 | tf_op jit(solution)/shard_map/ppermute | solution.py:626
  63.9 17.8 %copy-start.7 = (bf16[384,768]{1,0:T(8,128)(2,1)}, bf16[384,768]{1,0:T(8,128)(2,1)S(1)}, u32[]{:S(2)}) copy-start(bf16[384,768]{1,0:T(8,128)(2,1)S(1)} %constant_dynamic-update-slice_fusion.2.wo_a) | copy-start | bytes 1769476
  63.9 4.3 %collective-permute-start.3 = (bf16[384,768]{1,0:T(8,128)(2,1)S(1)}, bf16[384,768]{1,0:T(8,128)(2,1)S(1)}, u32[]{:S(2)}, u32[]{:S(2)}) collective-permute-start(bf16[384,768]{1,0:T(8,128)(2,1)S(1)} %constant_dynamic-update-slice_fusion.2.wo_a), channel_id=1, source_target_pairs={{0,1},{1,0},{2,3},{3,2},{4,5},{5,4},{6,7},{7,6},{8,9},{9,8},{10,11... | collective-permute-start | bytes 1769480 | tf_op jit(solution)/shard_map/ppermute | solution.py:626
  100.7 3.1 %collective-permute-start.7 = (bf16[768,768]{1,0:T(8,128)(2,1)}, bf16[768,768]{1,0:T(8,128)(2,1)S(1)}, u32[]{:S(2)}, u32[]{:S(2)}) collective-permute-start(bf16[768,768]{1,0:T(8,128)(2,1)} %get-tuple-element.66), channel_id=1, source_target_pairs={{0,1},{1,0},{2,3},{3,2},{4,5},{5,4},{6,7},{7,6},{8,9},{9,8},{10,11... | collective-permute-start | bytes 3538952 | tf_op jit(solution)/shard_map/ppermute | solution.py:626
  105.5 28.1 %copy-start.2 = (bf16[768,768]{1,0:T(8,128)(2,1)}, bf16[768,768]{1,0:T(8,128)(2,1)S(1)}, u32[]{:S(2)}) copy-start(bf16[768,768]{1,0:T(8,128)(2,1)S(1)} %add_convert_fusion.2.mine_ref) | copy-start | bytes 3538948
  105.5 28.1 %collective-permute-start.8 = (bf16[768,768]{1,0:T(8,128)(2,1)S(1)}, bf16[768,768]{1,0:T(8,128)(2,1)S(1)}, u32[]{:S(2)}, u32[]{:S(2)}) collective-permute-start(bf16[768,768]{1,0:T(8,128)(2,1)S(1)} %add_convert_fusion.2.mine_ref), channel_id=1, source_target_pairs={{0,2},{1,3},{2,0},{3,1},{4,6},{5,7},{6,4},{7,5},{8,10},{9,11},{10,... | collective-permute-start | bytes 3538952 | tf_op jit(solution)/shard_map/ppermute | solution.py:626
  141.4 3.1 %collective-permute-start.10 = (bf16[768,768]{1,0:T(8,128)(2,1)}, bf16[768,768]{1,0:T(8,128)(2,1)S(1)}, u32[]{:S(2)}, u32[]{:S(2)}) collective-permute-start(bf16[768,768]{1,0:T(8,128)(2,1)} %get-tuple-element.69.near_ref.skip_ref), channel_id=1, source_target_pairs={{0,1},{1,0},{2,3},{3,2},{4,5},{5,4},{6,7},{7,6},{8,9},{9,8},{10,11... | collective-permute-start | bytes 3538952 | tf_op jit(solution)/shard_map/ppermute | solution.py:626
  155.5 3.1 collective-permute-start.11
  160.2 28.1 %collective-permute-start.12 = (bf16[768,768]{1,0:T(8,128)(2,1)S(1)}, bf16[768,768]{1,0:T(8,128)(2,1)S(1)}, u32[]{:S(2)}, u32[]{:S(2)}) collective-permute-start(bf16[768,768]{1,0:T(8,128)(2,1)S(1)} %add_convert_fusion.1.mine_ref), channel_id=1, source_target_pairs={{0,2},{1,3},{2,0},{3,1},{4,6},{5,7},{6,4},{7,5},{8,10},{9,11},{10,... | collective-permute-start | bytes 3538952 | tf_op jit(solution)/shard_map/ppermute | solution.py:626
  170.9 28.0 %collective-permute-start.26 = (bf16[4,2,96,768]{3,2,1,0:T(8,128)(2,1)}, bf16[4,2,96,768]{3,2,1,0:T(8,128)(2,1)S(1)}, u32[]{:S(2)}, u32[]{:S(2)}) collective-permute-start(bf16[4,2,96,768]{3,2,1,0:T(8,128)(2,1)} %get-tuple-element.101), channel_id=1, source_target_pairs={{0,4},{4,0},{8,12},{12,8},{16,20},{20,16},{24,28},{28,24},{1,5},{5... | collective-permute-start | bytes 3538952 | tf_op jit(solution)/shard_map/ppermute | solution.py:626
  194.6 6.3 %collective-permute-start.13 = (bf16[768,768]{1,0:T(8,128)(2,1)}, bf16[768,768]{1,0:T(8,128)(2,1)S(1)}, u32[]{:S(2)}, u32[]{:S(2)}) collective-permute-start(bf16[768,768]{1,0:T(8,128)(2,1)} %get-tuple-element.75.near_ref), channel_id=1, source_target_pairs={{0,1},{1,0},{2,3},{3,2},{4,5},{5,4},{6,7},{7,6},{8,9},{9,8},{10,11... | collective-permute-start | bytes 3538952 | tf_op jit(solution)/shard_map/ppermute | solution.py:626
  194.6 47.8 %collective-permute-start.9 = (bf16[768,768]{1,0:T(8,128)(2,1)S(1)}, bf16[768,768]{1,0:T(8,128)(2,1)S(1)}, u32[]{:S(2)}, u32[]{:S(2)}) collective-permute-start(bf16[768,768]{1,0:T(8,128)(2,1)S(1)} %copy-done.9), channel_id=1, source_target_pairs={{0,1},{1,0},{2,3},{3,2},{4,5},{5,4},{6,7},{7,6},{8,9},{9,8},{10,11... | collective-permute-start | bytes 3538952 | tf_op jit(solution)/shard_map/ppermute | solution.py:626
  199.2 49.2 %collective-permute-start.27 = (bf16[2,2,96,768]{3,2,1,0:T(8,128)(2,1)S(1)}, bf16[2,2,96,768]{3,2,1,0:T(8,128)(2,1)S(1)}, u32[]{:S(2)}, u32[]{:S(2)}) collective-permute-start(bf16[2,2,96,768]{3,2,1,0:T(8,128)(2,1)S(1)} %split.37), channel_id=1, source_target_pairs={{0,8},{4,12},{8,0},{12,4},{16,24},{20,28},{24,16},{28,20},{1,9},{5... | collective-permute-start | bytes 1769480 | tf_op jit(solution)/shard_map/ppermute | solution.py:626
  239.7 14.1 %collective-permute-start.16 = (bf16[4,96,768]{2,1,0:T(8,128)(2,1)}, bf16[4,96,768]{2,1,0:T(8,128)(2,1)S(1)}, u32[]{:S(2)}, u32[]{:S(2)}) collective-permute-start(bf16[4,96,768]{2,1,0:T(8,128)(2,1)} %get-tuple-element.88), channel_id=1, source_target_pairs={{0,4},{4,0},{8,12},{12,8},{16,20},{20,16},{24,28},{28,24},{1,5},{5... | collective-permute-start | bytes 1769480 | tf_op jit(solution)/shard_map/ppermute | solution.py:626
  248.6 27.6 %collective-permute-start.28 = (bf16[1,2,96,768]{3,2,1,0:T(8,128)(2,1)S(1)}, bf16[1,2,96,768]{3,2,1,0:T(8,128)(2,1)S(1)}, u32[]{:S(2)}, u32[]{:S(2)}) collective-permute-start(bf16[1,2,96,768]{3,2,1,0:T(8,128)(2,1)S(1)} %split.39), channel_id=1, source_target_pairs={{0,16},{4,20},{8,24},{12,28},{16,0},{20,4},{24,8},{28,12},{1,17},{... | collective-permute-start | bytes 884744 | tf_op jit(solution)/shard_map/ppermute | solution.py:626
  249.1 5.6 %collective-permute-start.22 = (f32[6,768]{1,0:T(8,128)S(1)}, f32[6,768]{1,0:T(8,128)S(1)}, u32[]{:S(2)}, u32[]{:S(2)}) collective-permute-start(f32[6,768]{1,0:T(8,128)S(1)} %pad_maximum_fusion.4), channel_id=1, source_target_pairs={{0,1},{1,0},{2,3},{3,2},{4,5},{5,4},{6,7},{7,6},{8,9},{9,8},{10,11... | collective-permute-start | bytes 55304 | tf_op jit(solution)/shard_map/ppermute | solution.py:626
  254.0 12.9 %collective-permute-start.17 = (bf16[2,96,768]{2,1,0:T(8,128)(2,1)S(1)}, bf16[2,96,768]{2,1,0:T(8,128)(2,1)S(1)}, u32[]{:S(2)}, u32[]{:S(2)}) collective-permute-start(bf16[2,96,768]{2,1,0:T(8,128)(2,1)S(1)} %split.33), channel_id=1, source_target_pairs={{0,8},{4,12},{8,0},{12,4},{16,24},{20,28},{24,16},{28,20},{1,9},{5... | collective-permute-start | bytes 884744 | tf_op jit(solution)/shard_map/ppermute | solution.py:626
  261.1 21.1 %collective-permute-start.14 = (bf16[2,192,1536]{2,1,0:T(8,128)(2,1)}, bf16[2,192,1536]{2,1,0:T(8,128)(2,1)S(1)}, u32[]{:S(2)}, u32[]{:S(2)}) collective-permute-start(bf16[2,192,1536]{2,1,0:T(8,128)(2,1)} %get-tuple-element.84), channel_id=1, source_target_pairs={{0,1},{1,0},{2,3},{3,2},{4,5},{5,4},{6,7},{7,6},{8,9},{9,8},{10,11... | collective-permute-start | bytes 3538952 | tf_op jit(solution)/shard_map/ppermute | solution.py:626
  261.1 5.9 %collective-permute-start.23 = (f32[8,768]{1,0:T(8,128)S(1)}, f32[8,768]{1,0:T(8,128)S(1)}, u32[]{:S(2)}, u32[]{:S(2)}) collective-permute-start(f32[8,768]{1,0:T(8,128)S(1)} %select_maximum_fusion), channel_id=1, source_target_pairs={{0,4},{4,0},{8,12},{12,8},{16,20},{20,16},{24,28},{28,24},{1,5},{5... | collective-permute-start | bytes 73736 | tf_op jit(solution)/shard_map/ppermute | solution.py:626
  267.0 9.0 %collective-permute-start.18 = (bf16[1,96,768]{2,1,0:T(8,128)(2,1)S(1)}, bf16[1,96,768]{2,1,0:T(8,128)(2,1)S(1)}, u32[]{:S(2)}, u32[]{:S(2)}) collective-permute-start(bf16[1,96,768]{2,1,0:T(8,128)(2,1)S(1)} %split.35), channel_id=1, source_target_pairs={{0,16},{4,20},{8,24},{12,28},{16,0},{20,4},{24,8},{28,12},{1,17},{... | collective-permute-start | bytes 442376 | tf_op jit(solution)/shard_map/ppermute | solution.py:626
  267.1 9.1 %collective-permute-start.24 = (f32[8,768]{1,0:T(8,128)S(1)}, f32[8,768]{1,0:T(8,128)S(1)}, u32[]{:S(2)}, u32[]{:S(2)}) collective-permute-start(f32[8,768]{1,0:T(8,128)S(1)} %fusion.6), channel_id=1, source_target_pairs={{0,8},{4,12},{8,0},{12,4},{16,24},{20,28},{24,16},{28,20},{1,9},{5... | collective-permute-start | bytes 73736 | tf_op jit(solution)/shard_map/ppermute | solution.py:626
  276.0 6.1 %collective-permute-start.19 = (bf16[1,96,768]{2,1,0:T(8,128)(2,1)S(1)}, bf16[1,96,768]{2,1,0:T(8,128)(2,1)S(1)}, u32[]{:S(2)}, u32[]{:S(2)}) collective-permute-start(bf16[1,96,768]{2,1,0:T(8,128)(2,1)S(1)} %add_convert_fusion.6), channel_id=1, source_target_pairs={{0,16},{4,20},{8,24},{12,28},{16,0},{20,4},{24,8},{28,12},{1,17},{... | collective-permute-start | bytes 442376 | tf_op jit(solution)/shard_map/ppermute | solution.py:626
  276.2 10.5 %collective-permute-start.25 = (f32[8,768]{1,0:T(8,128)S(1)}, f32[8,768]{1,0:T(8,128)S(1)}, u32[]{:S(2)}, u32[]{:S(2)}) collective-permute-start(f32[8,768]{1,0:T(8,128)S(1)} %add.62), channel_id=1, source_target_pairs={{0,16},{4,20},{8,24},{12,28},{16,0},{20,4},{24,8},{28,12},{1,17},{... | collective-permute-start | bytes 73736 | tf_op jit(solution)/shard_map/ppermute | solution.py:626
  282.2 6.8 %collective-permute-start.20 = (bf16[2,96,768]{2,1,0:T(8,128)(2,1)S(1)}, bf16[2,96,768]{2,1,0:T(8,128)(2,1)S(1)}, u32[]{:S(2)}, u32[]{:S(2)}) collective-permute-start(bf16[2,96,768]{2,1,0:T(8,128)(2,1)S(1)} %pad_maximum_fusion.3), channel_id=1, source_target_pairs={{0,8},{4,12},{8,0},{12,4},{16,24},{20,28},{24,16},{28,20},{1,9},{5... | collective-permute-start | bytes 884744 | tf_op jit(solution)/shard_map/ppermute | solution.py:626
  282.7 16.6 %collective-permute-start.15 = (bf16[192,1536]{1,0:T(8,128)(2,1)S(1)}, bf16[192,1536]{1,0:T(8,128)(2,1)S(1)}, u32[]{:S(2)}, u32[]{:S(2)}) collective-permute-start(bf16[192,1536]{1,0:T(8,128)(2,1)S(1)} %fusion.3), channel_id=1, source_target_pairs={{0,2},{1,3},{2,0},{3,1},{4,6},{5,7},{6,4},{7,5},{8,10},{9,11},{10,... | collective-permute-start | bytes 1769480 | tf_op jit(solution)/shard_map/ppermute | solution.py:626
  289.0 13.3 %collective-permute-start.21 = (bf16[4,96,768]{2,1,0:T(8,128)(2,1)S(1)}, bf16[4,96,768]{2,1,0:T(8,128)(2,1)S(1)}, u32[]{:S(2)}, u32[]{:S(2)}) collective-permute-start(bf16[4,96,768]{2,1,0:T(8,128)(2,1)S(1)} %pad_maximum_fusion.2.near_ref), channel_id=1, source_target_pairs={{0,4},{4,0},{8,12},{12,8},{16,20},{20,16},{24,28},{28,24},{1,5},{5... | collective-permute-start | bytes 1769480 | tf_op jit(solution)/shard_map/ppermute | solution.py:626
  (28 other events, 173.4 us)
